TPU v7x, 256 devices: a whole 4x4x8 slice. The times are simulated.
256 devices in a mesh: dp: 2 (over x_hi), row: 16 (over z, core), col: 8 (over x_lo, y).
Axes of the slice: x: 4 (x_hi: 2, x_lo: 2; x = x_hi * 2 + x_lo), y: 4, z: 8, core: 2. Of those that a mesh axis runs over, the one named last changes fastest.
Arguments:
- tokens: bfloat16 [2048, 6144], P(('dp', 'col'), 'row'), may hold values from -6 to 6
- w_up: bfloat16 [6144, 24576], P('row', 'col'), may hold values from -0.078125 to 0.078125
- cotangent: bfloat16 [2048, 24576], P(('dp', 'row'), 'col'), may hold values from -6 to 6
Outputs:
- hidden: bfloat16 [2048, 24576], P(('dp', 'row'), 'col')
- weight_grad: float32 [6144, 24576], P('row', ('col', 'dp'))
- input_grad: bfloat16 [2048, 6144], P(('dp', 'col'), 'row')
All inputs are finite; a program needn't handle non-finite values.
Results may differ from a plain program's by a relative error of at most 0.025.
Values may be sent and summed in bfloat16 or wider, within the bound.
No kernel may reach another device: no remote copies, remote signals or barrier semaphores. Data moves between devices by JAX's collectives and lax.ppermute only.
A program may use at most 128 MiB of HBM per device.

v0:
```python
import jax
import jax.numpy as jnp
from jax import lax
from jax.experimental import pallas as pl
from jax.experimental.pallas import tpu as pltpu
from jax.sharding import Mesh, PartitionSpec as P

AXES = ("dp", "z", "core", "xl", "y")
SWAP = [(0, 1), (1, 0)]
BF16, F32 = jnp.bfloat16, jnp.float32
SQRT_2_PI = (2.0 / 3.141592653589793) ** 0.5
ROWS_COLS, BY_ROWS = ((1,), (0,)), ((0,), (0,))
VMEM = pl.BlockSpec(memory_space=pltpu.VMEM)
SMEM = pl.BlockSpec(memory_space=pltpu.SMEM)
PARAMS = dict(
    compiler_params=pltpu.CompilerParams(vmem_limit_bytes=32 << 20),
    cost_estimate=pl.CostEstimate(flops=1, bytes_accessed=1, transcendentals=0),
)


def cut(value, start, size, axis=0):
    return lax.dynamic_slice_in_dim(value, start, size, axis)


def dot(a, b, over):
    return lax.dot_general(a, b, (over, ((), ())), preferred_element_type=F32)


def after(value, *needed):
    return lax.optimization_barrier((value, needed))[0]


def row_blocks(panel, tables, counts, part):
    def body(table, panel, *outs):
        at = 0
        for out, count in zip(outs, counts):
            for i in range(count):
                start = pl.multiple_of(table[at] * part, part)
                out[i * part : (i + 1) * part] = panel[pl.ds(start, part), :]
                at += 1

    return pl.pallas_call(
        body,
        in_specs=[SMEM, VMEM],
        out_specs=[VMEM] * len(counts),
        out_shape=[jax.ShapeDtypeStruct((n * part, panel.shape[1]), panel.dtype) for n in counts],
        **PARAMS,
    )(tables, panel)


def activate(term, mine, theirs, cotangent, half, hidden=None):
    rows, cols = theirs.shape
    steps = 3
    tile = cols // steps
    last = term.shape[0] // rows - 1

    def body(half, term, mine, theirs, cot, *refs):
        hidden, grad = refs[-2:]
        v = term[...] + mine[...].astype(F32) + theirs[...].astype(F32)
        sq = v * v
        t = jnp.tanh(SQRT_2_PI * (v + 0.044715 * (sq * v)))
        hidden[...] = (0.5 * v * (1.0 + t)).astype(BF16)
        slope = 0.5 * (1.0 + t) + 0.5 * v * (1.0 - t * t) * (
            SQRT_2_PI * (1.0 + 3 * 0.044715 * sq)
        )
        grad[...] = (cot[...].astype(F32) * slope).astype(BF16)

    near = pl.BlockSpec((rows, tile), lambda i, half: (0, i))
    wide = pl.BlockSpec((rows, tile), lambda i, half: (0, half[0] * steps + i))
    more = () if hidden is None else (hidden,)
    return pl.pallas_call(
        body,
        grid_spec=pltpu.PrefetchScalarGridSpec(
            num_scalar_prefetch=1,
            grid=(steps,),
            in_specs=[pl.BlockSpec((rows, tile), lambda i, half: (last, i)), near, near, wide]
            + [pl.BlockSpec(memory_space=pl.ANY)] * len(more),
            out_specs=[wide, near],
        ),
        out_shape=[
            jax.ShapeDtypeStruct(cotangent.shape, BF16),
            jax.ShapeDtypeStruct((rows, cols), BF16),
        ],
        input_output_aliases={} if hidden is None else {5: 0},
        **PARAMS,
    )(half.reshape(1), term, mine, theirs, cotangent, *more)


def stacked(blocks):
    part, cols = blocks[0].shape
    tile = cols // 3

    def body(*refs):
        for i, r in enumerate(refs[:-1]):
            refs[-1][i * part : (i + 1) * part] = r[...]

    return pl.pallas_call(
        body,
        grid=(3,),
        in_specs=[pl.BlockSpec((part, tile), lambda i: (0, i))] * len(blocks),
        out_specs=pl.BlockSpec((part * len(blocks), tile), lambda i: (0, i)),
        out_shape=jax.ShapeDtypeStruct((part * len(blocks), cols), BF16),
        **PARAMS,
    )(*blocks)


def copies(value, count):
    def body(value, out):
        for i in range(count):
            out[i] = value[...]

    return pl.pallas_call(
        body,
        in_specs=[VMEM],
        out_specs=VMEM,
        out_shape=jax.ShapeDtypeStruct((count,) + value.shape, value.dtype),
        **PARAMS,
    )(value)


def rounded_sum(here, there):
    rows, cols = here.shape
    steps = 3
    tile = cols // steps

    def body(here, there, *outs):
        total = (here[...] + there[...].astype(F32)).astype(BF16)
        outs[0][...] = total[: rows // 2]
        outs[1][...] = total[rows // 2 :]

    wide = pl.BlockSpec((rows, tile), lambda i: (0, i))
    half = pl.BlockSpec((rows // 2, tile), lambda i: (0, i))
    return pl.pallas_call(
        body,
        grid=(steps,),
        in_specs=[wide, wide],
        out_specs=[half, half],
        out_shape=[jax.ShapeDtypeStruct((rows // 2, cols), BF16)] * 2,
        **PARAMS,
    )(here, there)


def scaled_sum(here, there, sent, scale, which, out=None):
    rows, cols = here.shape
    steps = 3
    tile = rows // 2 // steps

    def body(here, there, sent, *refs):
        total = here[...] + there[...].astype(F32) + sent[...].astype(F32)
        refs[-1][...] = total * scale

    spec = pl.BlockSpec((tile, cols), lambda i: (i + which * steps, 0))
    more = () if out is None else (out,)
    return pl.pallas_call(
        body,
        grid=(steps,),
        in_specs=[spec, spec, pl.BlockSpec((tile, cols), lambda i: (i, 0))]
        + [pl.BlockSpec(memory_space=pl.ANY)] * len(more),
        out_specs=spec,
        out_shape=jax.ShapeDtypeStruct((rows, cols), F32),
        input_output_aliases={} if out is None else {3: 0},
        **PARAMS,
    )(here, there, sent, *more)


def by_y(here, there, scalars, rows, ny):
    part, depth = rows // 2, here.shape[1]

    def body(s, here, there, *outs):
        first = s[0] == 0

        def own(hop):
            return jnp.where(hop < 2, hop * part, (hop - 1) * rows)

        def other(hop):
            return part + hop * rows

        def take(low, start):
            start = pl.ds(pl.multiple_of(start, part), part)
            return jnp.where(first == low, here[start, :], there[start, :])

        for hop, out in enumerate(outs):
            k = lax.rem(s[1] + hop, ny)
            edge = k == 0
            up = ny - k
            out[0, :part] = take(edge, jnp.where(edge, 0, other(k)))
            out[0, part:] = take(False, own(k))
            out[1, :part] = take(True, own(up))
            out[1, part:] = take(jnp.logical_not(edge), jnp.where(edge, own(up), other(up)))

    return pl.pallas_call(
        body,
        in_specs=[SMEM, VMEM, VMEM],
        out_specs=[VMEM] * ny,
        out_shape=[jax.ShapeDtypeStruct((2, rows, depth), BF16)] * ny,
        **PARAMS,
    )(scalars, here, there)


def shards(tokens, w_up, cotangent):
    nz, ny = lax.axis_size("z"), lax.axis_size("y")
    ncol = lax.axis_size("xl") * ny
    half_z = nz // 2
    d, z, c, xl, y = (lax.axis_index(name) for name in AXES)
    rows, depth = tokens.shape
    part = rows // 2
    cols = w_up.shape[1] // 2
    step = 1 - 2 * c
    ring = [(2 * i, 2 * ((i + 1) % nz)) for i in range(nz)] + [
        (2 * i + 1, 2 * ((i - 1) % nz) + 1) for i in range(nz)
    ]

    def swap(value):
        return lax.ppermute(value, "core", SWAP)

    def along(value):
        return lax.ppermute(value, ("z", "core"), ring)

    def halves(value):
        return (cut(value, (1 - d) * cols, cols, 1), cut(value, d * cols, cols, 1))

    def place(hop):
        return (z + hop + nz) % nz

    w_other = swap(w_up)
    weights = [
        jnp.concatenate(pair, 0) for pair in zip(halves(w_up), halves(w_other))
    ]
    panel = lax.all_to_all(
        copies(tokens, ncol), ("xl", "y"), 0, 0
    ).reshape(ncol * rows, depth)
    panel, weights = lax.optimization_barrier((panel, weights))

    def near_table(sign, half):
        out = []
        for hop in range(half_z - 1, 0, -1):
            out += [2 * place(sign * hop) + half, 2 * place(sign * hop) + 1 - half]
        return out + [2 * z + half]

    table = [2 * place(half_z) + c, 2 * place(half_z) + 1 - c]
    table += near_table(step, c) + near_table(-step, 1 - c)
    count = 2 * half_z - 1
    far, far_send, ahead, behind = row_blocks(
        panel, jnp.stack(table).astype(jnp.int32), (1, 1, count, count), part
    )
    x_far = jnp.concatenate([far, swap(far_send)], 1)
    x_ahead = jnp.concatenate([ahead, swap(behind)], 1)
    first_terms, terms = [], []
    for w in weights:
        x = after(x_far, terms[-1]) if terms else x_far
        first_terms.append(dot(x, w, ROWS_COLS).astype(BF16))
        terms.append(dot(x_ahead, w, ROWS_COLS))
    first = [along(t) for t in first_terms]

    held, sent = list(first), first_terms[1]
    for i in range(half_z - 1):
        held[0] = after(held[0], sent)
        for n, t in enumerate(terms):
            h = held[n] if i else jnp.pad(held[n], ((0, part), (0, 0)))
            sent = (t[i * rows : (i + 1) * rows] + h.astype(F32)).astype(BF16)
            held[n] = along(sent)
    held[0] = after(held[0], sent)
    hidden, grads = None, []
    for n, half in enumerate((1 - d, d)):
        if grads:
            held[n] = after(held[n], grads[0])
        hidden, g = activate(terms[n], held[n], swap(held[n][part:]), cotangent, half, hidden)
        grads.append(g)

    own, other = [[g] for g in grads], [[swap(g)] for g in grads]
    sent = grads[1]
    for hop in range(half_z):
        if hop > 0:
            own[0][hop] = after(own[0][hop], sent)
        for n in range(2):
            own[n].append(along(own[n][hop]))
            if hop > 0:
                other[n].append(along(other[n][hop - 1]))
        sent = (own[1][hop], other[1][max(hop - 1, 0)])
    own[0][half_z] = after(own[0][half_z], sent)
    blocks = []
    for n in range(2):
        got = own[n][:2]
        for hop in range(2, half_z + 1):
            got += [own[n][hop], other[n][hop - 1]]
        blocks.append(got)

    def back_table(sign, half):
        out = [2 * z + half, 2 * place(sign) + half]
        for hop in range(2, half_z + 1):
            out += [2 * place(sign * hop) + half, 2 * place(sign * (hop - 1)) + 1 - half]
        return out

    back, back_send = row_blocks(
        panel,
        jnp.stack(back_table(-step, c) + back_table(step, 1 - c)).astype(jnp.int32),
        (2 * half_z, 2 * half_z),
        part,
    )
    x_back = jnp.concatenate([back, swap(back_send)], 1)

    def weight_terms(block):
        there = swap(dot(x_back[:, depth:], block, BY_ROWS).astype(BF16))
        return dot(x_back[:, :depth], block, BY_ROWS), there

    to_peer = rounded_sum(*weight_terms(stacked(blocks[0])))
    sent = [lax.ppermute(p, "dp", SWAP) for p in to_peer]

    blocks = [stacked(after(b, to_peer)) for b in blocks]
    out = sum(dot(b, w, ((1,), (1,))) for b, w in zip(blocks, weights)).astype(BF16)
    here, there = out[:, :depth], swap(out[:, depth:])
    there = after(there, sent[0])
    scalars = jnp.stack([c, (y - z + nz) % ny]).astype(jnp.int32)
    for_y = by_y(here, there, scalars, rows, ny)
    own_terms = weight_terms(after(blocks[1], out))
    scale = float(nz * rows * lax.axis_size("dp")) ** (-0.5)
    weight_grad = scaled_sum(*own_terms, sent[0], scale, 0)
    total = for_y[0].astype(F32)
    for hop in range(1, ny):
        total += lax.ppermute(
            for_y[hop], "y", [(i, (i + hop) % ny) for i in range(ny)]
        ).astype(F32)
    total = after(total.astype(BF16), sent[1], weight_grad)
    weight_grad = scaled_sum(*own_terms, sent[1], scale, 1, weight_grad)
    mine = place((y - z + nz) % ny) // ny == xl
    keep, send = jnp.where(mine, total[0], total[1]), jnp.where(mine, total[1], total[0])
    input_grad = (
        keep.astype(F32) + lax.ppermute(send, "xl", SWAP).astype(F32)
    ).astype(BF16)
    return (hidden, weight_grad, input_grad)


def solution(mesh):
    fine = Mesh(mesh.devices.reshape(2, 8, 2, 2, 4), AXES)
    tokens_at = P(("dp", "xl", "y"), ("z", "core"))
    hidden_at = P(("dp", "z", "core"), ("xl", "y"))
    return jax.shard_map(
        shards,
        mesh=fine,
        in_specs=(tokens_at, P(("z", "core"), ("xl", "y")), hidden_at),
        out_specs=(hidden_at, P(("z", "core"), ("xl", "y", "dp")), tokens_at),
        check_vma=False,
    )
```

profile of v0, /device:TPU:4, one launch (start us, length us, event | category | flops | bytes accessed | tf_op | source)
XLA Modules:
  0.0 140.8 jit_solution(9142349069781350032)
XLA Ops:
  2.6 5.2 %all-to-all-start = ((bf16[8,128,384]{2,1,0:T(8,128)(2,1)}), bf16[8,128,384]{2,1,0:T(8,128)(2,1)S(1)}, u32[]{:S(2)}, u32[]{:S(2)}) async-start(bf16[8,128,384]{2,1,0:T(8,128)(2,1)} %shard_map.58), calls=%async_computation | async-start | bytes 1572864 | tf_op jit(solution)/shard_map/all_to_all | solution.py:229
  13.4 7.1 %all-to-all-done = bf16[8,128,384]{2,1,0:T(8,128)(2,1)S(1)} async-done(((bf16[8,128,384]{2,1,0:T(8,128)(2,1)}), bf16[8,128,384]{2,1,0:T(8,128)(2,1)S(1)}, u32[]{:S(2)}, u32[]{:S(2)}) %all-to-all-start) | async-done | bytes 786464 | tf_op jit(solution)/shard_map/all_to_all | solution.py:229
  22.9 2.0 %collective-permute-start.7 = (bf16[64,1536]{1,0:T(8,128)(2,1)S(1)}, bf16[64,1536]{1,0:T(8,128)(2,1)S(1)}, u32[]{:S(2)}, u32[]{:S(2)}) collective-permute-start(bf16[64,1536]{1,0:T(8,128)(2,1)S(1)} %convolution_convert_fusion.2), channel_id=1, source_target_pairs={{0,16},{16,32},{32,48},{48,64},{64,80},{80,96},{96,112},{112,0},{8... | collective-permute-start | bytes 589832 | tf_op jit(solution)/shard_map/ppermute | solution.py:217
  27.2 2.0 %collective-permute-start.3 = (bf16[64,1536]{1,0:T(8,128)(2,1)S(1)}, bf16[64,1536]{1,0:T(8,128)(2,1)S(1)}, u32[]{:S(2)}, u32[]{:S(2)}) collective-permute-start(bf16[64,1536]{1,0:T(8,128)(2,1)S(1)} %convolution_convert_fusion.3), channel_id=1, source_target_pairs={{0,16},{16,32},{32,48},{48,64},{64,80},{80,96},{96,112},{112,0},{8... | collective-permute-start | bytes 589832 | tf_op jit(solution)/shard_map/ppermute | solution.py:217
  29.2 3.3 %collective-permute-done.7 = bf16[64,1536]{1,0:T(8,128)(2,1)S(1)} collective-permute-done((bf16[64,1536]{1,0:T(8,128)(2,1)S(1)}, bf16[64,1536]{1,0:T(8,128)(2,1)S(1)}, u32[]{:S(2)}, u32[]{:S(2)}) %collective-permute-start.7) | collective-permute-done | bytes 196640 | tf_op jit(solution)/shard_map/ppermute | solution.py:217
  35.8 5.9 %collective-permute-done.8 = bf16[128,1536]{1,0:T(8,128)(2,1)S(1)} collective-permute-done((bf16[128,1536]{1,0:T(8,128)(2,1)S(1)}, bf16[128,1536]{1,0:T(8,128)(2,1)S(1)}, u32[]{:S(2)}, u32[]{:S(2)}) %collective-permute-start.8) | collective-permute-done | bytes 393248 | tf_op jit(solution)/shard_map/ppermute | solution.py:217
  41.8 4.0 %collective-permute-done.4 = bf16[128,1536]{1,0:T(8,128)(2,1)S(1)} collective-permute-done((bf16[128,1536]{1,0:T(8,128)(2,1)S(1)}, bf16[128,1536]{1,0:T(8,128)(2,1)S(1)}, u32[]{:S(2)}, u32[]{:S(2)}) %collective-permute-start.4) | collective-permute-done | bytes 393248 | tf_op jit(solution)/shard_map/ppermute | solution.py:217
  46.0 4.8 %collective-permute-done.9 = bf16[128,1536]{1,0:T(8,128)(2,1)S(1)} collective-permute-done((bf16[128,1536]{1,0:T(8,128)(2,1)S(1)}, bf16[128,1536]{1,0:T(8,128)(2,1)S(1)}, u32[]{:S(2)}, u32[]{:S(2)}) %collective-permute-start.9) | collective-permute-done | bytes 393248 | tf_op jit(solution)/shard_map/ppermute | solution.py:217
  51.0 4.0 %collective-permute-done.5 = bf16[128,1536]{1,0:T(8,128)(2,1)S(1)} collective-permute-done((bf16[128,1536]{1,0:T(8,128)(2,1)S(1)}, bf16[128,1536]{1,0:T(8,128)(2,1)S(1)}, u32[]{:S(2)}, u32[]{:S(2)}) %collective-permute-start.5) | collective-permute-done | bytes 393248 | tf_op jit(solution)/shard_map/ppermute | solution.py:217
  55.2 4.8 %collective-permute-done.10.mine = bf16[128,1536]{1,0:T(8,128)(2,1)S(1)} collective-permute-done((bf16[128,1536]{1,0:T(8,128)(2,1)S(1)}, bf16[128,1536]{1,0:T(8,128)(2,1)S(1)}, u32[]{:S(2)}, u32[]{:S(2)}) %collective-permute-start.10) | collective-permute-done | bytes 393248 | tf_op jit(solution)/shard_map/ppermute | solution.py:217
  69.0 2.3 %collective-permute-done.21.refs_1_ = bf16[64,1536]{1,0:T(8,128)(2,1)S(1)} collective-permute-done((bf16[64,1536]{1,0:T(8,128)(2,1)S(1)}, bf16[64,1536]{1,0:T(8,128)(2,1)S(1)}, u32[]{:S(2)}, u32[]{:S(2)}) %collective-permute-start.21) | collective-permute-done | bytes 196640 | tf_op jit(solution)/shard_map/ppermute | solution.py:217
  74.3 2.0 %collective-permute-done.24.refs_3_ = bf16[64,1536]{1,0:T(8,128)(2,1)S(1)} collective-permute-done((bf16[64,1536]{1,0:T(8,128)(2,1)S(1)}, bf16[64,1536]{1,0:T(8,128)(2,1)S(1)}, u32[]{:S(2)}, u32[]{:S(2)}) %collective-permute-start.24) | collective-permute-done | bytes 196640 | tf_op jit(solution)/shard_map/ppermute | solution.py:217
  80.1 2.6 %collective-permute-done.14.refs_2_ = bf16[64,1536]{1,0:T(8,128)(2,1)S(1)} collective-permute-done((bf16[64,1536]{1,0:T(8,128)(2,1)S(1)}, bf16[64,1536]{1,0:T(8,128)(2,1)S(1)}, u32[]{:S(2)}, u32[]{:S(2)}) %collective-permute-start.14) | collective-permute-done | bytes 196640 | tf_op jit(solution)/shard_map/ppermute | solution.py:217
  84.7 2.2 %collective-permute-done.25.refs_4_ = bf16[64,1536]{1,0:T(8,128)(2,1)S(1)} collective-permute-done((bf16[64,1536]{1,0:T(8,128)(2,1)S(1)}, bf16[64,1536]{1,0:T(8,128)(2,1)S(1)}, u32[]{:S(2)}, u32[]{:S(2)}) %collective-permute-start.25) | collective-permute-done | bytes 196640 | tf_op jit(solution)/shard_map/ppermute | solution.py:217
  86.9 2.1 %collective-permute-start.28 = (bf16[64,1536]{1,0:T(8,128)(2,1)S(1)}, bf16[64,1536]{1,0:T(8,128)(2,1)S(1)}, u32[]{:S(2)}, u32[]{:S(2)}) collective-permute-start(bf16[64,1536]{1,0:T(8,128)(2,1)S(1)} %collective-permute-done.26.refs_5_), channel_id=1, source_target_pairs={{0,16},{16,32},{32,48},{48,64},{64,80},{80,96},{96,112},{112,0},{8... | collective-permute-start | bytes 589832 | tf_op jit(solution)/shard_map/ppermute | solution.py:217
  89.6 2.1 %collective-permute-done.18.refs_5_ = bf16[64,1536]{1,0:T(8,128)(2,1)S(1)} collective-permute-done((bf16[64,1536]{1,0:T(8,128)(2,1)S(1)}, bf16[64,1536]{1,0:T(8,128)(2,1)S(1)}, u32[]{:S(2)}, u32[]{:S(2)}) %collective-permute-start.18) | collective-permute-done | bytes 196640 | tf_op jit(solution)/shard_map/ppermute | solution.py:217
  91.7 2.1 %collective-permute-done.27.refs_6_ = bf16[64,1536]{1,0:T(8,128)(2,1)S(1)} collective-permute-done((bf16[64,1536]{1,0:T(8,128)(2,1)S(1)}, bf16[64,1536]{1,0:T(8,128)(2,1)S(1)}, u32[]{:S(2)}, u32[]{:S(2)}) %collective-permute-start.27) | collective-permute-done | bytes 196640 | tf_op jit(solution)/shard_map/ppermute | solution.py:217
  93.8 2.1 %collective-permute-done.28.refs_7_ = bf16[64,1536]{1,0:T(8,128)(2,1)S(1)} collective-permute-done((bf16[64,1536]{1,0:T(8,128)(2,1)S(1)}, bf16[64,1536]{1,0:T(8,128)(2,1)S(1)}, u32[]{:S(2)}, u32[]{:S(2)}) %collective-permute-start.28) | collective-permute-done | bytes 196640 | tf_op jit(solution)/shard_map/ppermute | solution.py:217
  104.2 2.1 %collective-permute-done.20.refs_7_ = bf16[64,1536]{1,0:T(8,128)(2,1)S(1)} collective-permute-done((bf16[64,1536]{1,0:T(8,128)(2,1)S(1)}, bf16[64,1536]{1,0:T(8,128)(2,1)S(1)}, u32[]{:S(2)}, u32[]{:S(2)}) %collective-permute-start.20) | collective-permute-done | bytes 196640 | tf_op jit(solution)/shard_map/ppermute | solution.py:217
  116.8 2.1 %collective-permute-done.33.sent = bf16[192,1536]{1,0:T(8,128)(2,1)} collective-permute-done((bf16[192,1536]{1,0:T(8,128)(2,1)}, bf16[192,1536]{1,0:T(8,128)(2,1)}, u32[]{:S(2)}, u32[]{:S(2)}) %collective-permute-start.33) | collective-permute-done | bytes 589856 | tf_op jit(solution)/shard_map/ppermute | solution.py:307
  121.0 2.1 %collective-permute-start.36 = (bf16[2,128,384]{2,1,0:T(8,128)(2,1)S(1)}, bf16[2,128,384]{2,1,0:T(8,128)(2,1)S(1)}, u32[]{:S(2)}, u32[]{:S(2)}) collective-permute-start(bf16[2,128,384]{2,1,0:T(8,128)(2,1)S(1)} %get-tuple-element.96), channel_id=1, source_target_pairs={{0,2},{1,3},{2,0},{3,1},{4,6},{5,7},{6,4},{7,5},{8,10},{9,11},{10,... | collective-permute-start | bytes 589832 | tf_op jit(solution)/shard_map/ppermute | solution.py:320
  125.4 6.3 %collective-permute-done.35 = bf16[2,128,384]{2,1,0:T(8,128)(2,1)S(1)} collective-permute-done((bf16[2,128,384]{2,1,0:T(8,128)(2,1)S(1)}, bf16[2,128,384]{2,1,0:T(8,128)(2,1)S(1)}, u32[]{:S(2)}, u32[]{:S(2)}) %collective-permute-start.35) | collective-permute-done | bytes 196640 | tf_op jit(solution)/shard_map/ppermute | solution.py:320
  132.4 3.0 %shard_map.67.refs_0_ = f32[384,1536]{1,0:T(8,128)} custom-call(f32[384,1536]{1,0:T(8,128)S(1)} %fusion.12.here, bf16[384,1536]{1,0:T(8,128)(2,1)S(1)} %collective-permute-done.31.there, bf16[192,1536]{1,0:T(8,128)(2,1)} %collective-permute-done.33.sent), custom_call_target="tpu_custom_call" | custom-call | flops 1 | bytes 1 | tf_op jit(solution)/shard_map/pallas_call | solution.py:154
  137.0 3.0 %shard_map.68 = f32[384,1536]{1,0:T(8,128)} custom-call(f32[384,1536]{1,0:T(8,128)S(1)} %fusion.12.here, bf16[384,1536]{1,0:T(8,128)(2,1)S(1)} %collective-permute-done.31.there, bf16[192,1536]{1,0:T(8,128)(2,1)} %collective-permute-done.32.sent, f32[384,1536]{1,0:T(8,128)} %shard_map.67.refs_0_), custom_call_target="tpu_custom_call", output_to_operand_aliasing={{}: (3, {})} | custom-call | flops 1 | bytes 1 | tf_op jit(solution)/shard_map/pallas_call | solution.py:154
  (128 shorter events, 60.6 us)
Async XLA Ops:
  0.6 8.9 %collective-permute-start = (bf16[384,3072]{1,0:T(8,128)(2,1)}, bf16[384,3072]{1,0:T(8,128)(2,1)}, u32[]{:S(2)}, u32[]{:S(2)}) collective-permute-start(bf16[384,3072]{1,0:T(8,128)(2,1)} %param.4), channel_id=1, source_target_pairs={{0,8},{8,0},{1,9},{9,1},{2,10},{10,2},{3,11},{11,3},{4,12},{12,4},... | collective-permute-start | bytes 7077896 | tf_op jit(solution)/shard_map/ppermute | solution.py:214
  2.6 17.9 %all-to-all-start = ((bf16[8,128,384]{2,1,0:T(8,128)(2,1)}), bf16[8,128,384]{2,1,0:T(8,128)(2,1)S(1)}, u32[]{:S(2)}, u32[]{:S(2)}) async-start(bf16[8,128,384]{2,1,0:T(8,128)(2,1)} %shard_map.58), calls=%async_computation | async-start | bytes 1572864 | tf_op jit(solution)/shard_map/all_to_all | solution.py:229
  22.9 9.6 %collective-permute-start.7 = (bf16[64,1536]{1,0:T(8,128)(2,1)S(1)}, bf16[64,1536]{1,0:T(8,128)(2,1)S(1)}, u32[]{:S(2)}, u32[]{:S(2)}) collective-permute-start(bf16[64,1536]{1,0:T(8,128)(2,1)S(1)} %convolution_convert_fusion.2), channel_id=1, source_target_pairs={{0,16},{16,32},{32,48},{48,64},{64,80},{80,96},{96,112},{112,0},{8... | collective-permute-start | bytes 589832 | tf_op jit(solution)/shard_map/ppermute | solution.py:217
  32.6 9.1 %collective-permute-start.8 = (bf16[128,1536]{1,0:T(8,128)(2,1)S(1)}, bf16[128,1536]{1,0:T(8,128)(2,1)S(1)}, u32[]{:S(2)}, u32[]{:S(2)}) collective-permute-start(bf16[128,1536]{1,0:T(8,128)(2,1)S(1)} %fusion), channel_id=1, source_target_pairs={{0,16},{16,32},{32,48},{48,64},{64,80},{80,96},{96,112},{112,0},{8... | collective-permute-start | bytes 1179656 | tf_op jit(solution)/shard_map/ppermute | solution.py:217
  35.0 10.9 %collective-permute-start.4 = (bf16[128,1536]{1,0:T(8,128)(2,1)S(1)}, bf16[128,1536]{1,0:T(8,128)(2,1)S(1)}, u32[]{:S(2)}, u32[]{:S(2)}) collective-permute-start(bf16[128,1536]{1,0:T(8,128)(2,1)S(1)} %fusion.3), channel_id=1, source_target_pairs={{0,16},{16,32},{32,48},{48,64},{64,80},{80,96},{96,112},{112,0},{8... | collective-permute-start | bytes 1179656 | tf_op jit(solution)/shard_map/ppermute | solution.py:217
  41.7 9.1 %collective-permute-start.9 = (bf16[128,1536]{1,0:T(8,128)(2,1)S(1)}, bf16[128,1536]{1,0:T(8,128)(2,1)S(1)}, u32[]{:S(2)}, u32[]{:S(2)}) collective-permute-start(bf16[128,1536]{1,0:T(8,128)(2,1)S(1)} %fusion.1), channel_id=1, source_target_pairs={{0,16},{16,32},{32,48},{48,64},{64,80},{80,96},{96,112},{112,0},{8... | collective-permute-start | bytes 1179656 | tf_op jit(solution)/shard_map/ppermute | solution.py:217
  45.9 9.1 %collective-permute-start.5 = (bf16[128,1536]{1,0:T(8,128)(2,1)S(1)}, bf16[128,1536]{1,0:T(8,128)(2,1)S(1)}, u32[]{:S(2)}, u32[]{:S(2)}) collective-permute-start(bf16[128,1536]{1,0:T(8,128)(2,1)S(1)} %fusion.4), channel_id=1, source_target_pairs={{0,16},{16,32},{32,48},{48,64},{64,80},{80,96},{96,112},{112,0},{8... | collective-permute-start | bytes 1179656 | tf_op jit(solution)/shard_map/ppermute | solution.py:217
  50.9 9.1 %collective-permute-start.10 = (bf16[128,1536]{1,0:T(8,128)(2,1)S(1)}, bf16[128,1536]{1,0:T(8,128)(2,1)S(1)}, u32[]{:S(2)}, u32[]{:S(2)}) collective-permute-start(bf16[128,1536]{1,0:T(8,128)(2,1)S(1)} %fusion.2), channel_id=1, source_target_pairs={{0,16},{16,32},{32,48},{48,64},{64,80},{80,96},{96,112},{112,0},{8... | collective-permute-start | bytes 1179656 | tf_op jit(solution)/shard_map/ppermute | solution.py:217
  55.1 9.1 %collective-permute-start.6 = (bf16[128,1536]{1,0:T(8,128)(2,1)S(1)}, bf16[128,1536]{1,0:T(8,128)(2,1)S(1)}, u32[]{:S(2)}, u32[]{:S(2)}) collective-permute-start(bf16[128,1536]{1,0:T(8,128)(2,1)S(1)} %fusion.5), channel_id=1, source_target_pairs={{0,16},{16,32},{32,48},{48,64},{64,80},{80,96},{96,112},{112,0},{8... | collective-permute-start | bytes 1179656 | tf_op jit(solution)/shard_map/ppermute | solution.py:217
  68.1 8.3 %collective-permute-start.24 = (bf16[64,1536]{1,0:T(8,128)(2,1)S(1)}, bf16[64,1536]{1,0:T(8,128)(2,1)S(1)}, u32[]{:S(2)}, u32[]{:S(2)}) collective-permute-start(bf16[64,1536]{1,0:T(8,128)(2,1)S(1)} %collective-permute-done.23), channel_id=1, source_target_pairs={{0,16},{16,32},{32,48},{48,64},{64,80},{80,96},{96,112},{112,0},{8... | collective-permute-start | bytes 589832 | tf_op jit(solution)/shard_map/ppermute | solution.py:217
  72.7 10.0 %collective-permute-start.16 = (bf16[64,1536]{1,0:T(8,128)(2,1)S(1)}, bf16[64,1536]{1,0:T(8,128)(2,1)S(1)}, u32[]{:S(2)}, u32[]{:S(2)}) collective-permute-start(bf16[64,1536]{1,0:T(8,128)(2,1)S(1)} %collective-permute-done.15), channel_id=1, source_target_pairs={{0,16},{16,32},{32,48},{48,64},{64,80},{80,96},{96,112},{112,0},{8... | collective-permute-start | bytes 589832 | tf_op jit(solution)/shard_map/ppermute | solution.py:217
  74.2 8.4 %collective-permute-start.14 = (bf16[64,1536]{1,0:T(8,128)(2,1)S(1)}, bf16[64,1536]{1,0:T(8,128)(2,1)S(1)}, u32[]{:S(2)}, u32[]{:S(2)}) collective-permute-start(bf16[64,1536]{1,0:T(8,128)(2,1)S(1)} %collective-permute-done.13.refs_1_), channel_id=1, source_target_pairs={{0,16},{16,32},{32,48},{48,64},{64,80},{80,96},{96,112},{112,0},{8... | collective-permute-start | bytes 589832 | tf_op jit(solution)/shard_map/ppermute | solution.py:217
  76.4 10.5 %collective-permute-start.26 = (bf16[64,1536]{1,0:T(8,128)(2,1)S(1)}, bf16[64,1536]{1,0:T(8,128)(2,1)S(1)}, u32[]{:S(2)}, u32[]{:S(2)}) collective-permute-start(bf16[64,1536]{1,0:T(8,128)(2,1)S(1)} %collective-permute-done.24.refs_3_), channel_id=1, source_target_pairs={{0,16},{16,32},{32,48},{48,64},{64,80},{80,96},{96,112},{112,0},{8... | collective-permute-start | bytes 589832 | tf_op jit(solution)/shard_map/ppermute | solution.py:217
  78.5 8.4 %collective-permute-start.25 = (bf16[64,1536]{1,0:T(8,128)(2,1)S(1)}, bf16[64,1536]{1,0:T(8,128)(2,1)S(1)}, u32[]{:S(2)}, u32[]{:S(2)}) collective-permute-start(bf16[64,1536]{1,0:T(8,128)(2,1)S(1)} %collective-permute-done.22.refs_2_), channel_id=1, source_target_pairs={{0,16},{16,32},{32,48},{48,64},{64,80},{80,96},{96,112},{112,0},{8... | collective-permute-start | bytes 589832 | tf_op jit(solution)/shard_map/ppermute | solution.py:217
  79.2 17.1 %collective-permute-start.29 = (bf16[512,384]{1,0:T(8,128)(2,1)S(1)}, bf16[512,384]{1,0:T(8,128)(2,1)S(1)}, u32[]{:S(2)}, u32[]{:S(2)}) collective-permute-start(bf16[512,384]{1,0:T(8,128)(2,1)S(1)} %get-tuple-element.73), channel_id=1, source_target_pairs={{0,8},{8,0},{1,9},{9,1},{2,10},{10,2},{3,11},{11,3},{4,12},{12,4},... | collective-permute-start | bytes 1179656 | tf_op jit(solution)/shard_map/ppermute | solution.py:214
  82.7 9.0 %collective-permute-start.18 = (bf16[64,1536]{1,0:T(8,128)(2,1)S(1)}, bf16[64,1536]{1,0:T(8,128)(2,1)S(1)}, u32[]{:S(2)}, u32[]{:S(2)}) collective-permute-start(bf16[64,1536]{1,0:T(8,128)(2,1)S(1)} %collective-permute-done.16.refs_3_), channel_id=1, source_target_pairs={{0,16},{16,32},{32,48},{48,64},{64,80},{80,96},{96,112},{112,0},{8... | collective-permute-start | bytes 589832 | tf_op jit(solution)/shard_map/ppermute | solution.py:217
  86.9 9.0 %collective-permute-start.28 = (bf16[64,1536]{1,0:T(8,128)(2,1)S(1)}, bf16[64,1536]{1,0:T(8,128)(2,1)S(1)}, u32[]{:S(2)}, u32[]{:S(2)}) collective-permute-start(bf16[64,1536]{1,0:T(8,128)(2,1)S(1)} %collective-permute-done.26.refs_5_), channel_id=1, source_target_pairs={{0,16},{16,32},{32,48},{48,64},{64,80},{80,96},{96,112},{112,0},{8... | collective-permute-start | bytes 589832 | tf_op jit(solution)/shard_map/ppermute | solution.py:217
  97.3 9.0 %collective-permute-start.20 = (bf16[64,1536]{1,0:T(8,128)(2,1)S(1)}, bf16[64,1536]{1,0:T(8,128)(2,1)S(1)}, u32[]{:S(2)}, u32[]{:S(2)}) collective-permute-start(bf16[64,1536]{1,0:T(8,128)(2,1)S(1)} %collective-permute-done.18.refs_5_), channel_id=1, source_target_pairs={{0,16},{16,32},{32,48},{48,64},{64,80},{80,96},{96,112},{112,0},{8... | collective-permute-start | bytes 589832 | tf_op jit(solution)/shard_map/ppermute | solution.py:217
  101.8 17.2 %collective-permute-start.33 = (bf16[192,1536]{1,0:T(8,128)(2,1)}, bf16[192,1536]{1,0:T(8,128)(2,1)}, u32[]{:S(2)}, u32[]{:S(2)}) collective-permute-start(bf16[192,1536]{1,0:T(8,128)(2,1)} %get-tuple-element.74), channel_id=1, source_target_pairs={{0,128},{128,0},{1,129},{129,1},{2,130},{130,2},{3,131},{131,3},{4... | collective-permute-start | bytes 1769480 | tf_op jit(solution)/shard_map/ppermute | solution.py:307
  113.1 19.3 %collective-permute-start.31 = (bf16[384,1536]{1,0:T(8,128)(2,1)}, bf16[384,1536]{1,0:T(8,128)(2,1)S(1)}, u32[]{:S(2)}, u32[]{:S(2)}) collective-permute-start(bf16[384,1536]{1,0:T(8,128)(2,1)} %convolution_convert_fusion), channel_id=1, source_target_pairs={{0,8},{8,0},{1,9},{9,1},{2,10},{10,2},{3,11},{11,3},{4,12},{12,4},... | collective-permute-start | bytes 3538952 | tf_op jit(solution)/shard_map/ppermute | solution.py:214
  114.5 20.9 %collective-permute-start.32 = (bf16[192,1536]{1,0:T(8,128)(2,1)}, bf16[192,1536]{1,0:T(8,128)(2,1)}, u32[]{:S(2)}, u32[]{:S(2)}) collective-permute-start(bf16[192,1536]{1,0:T(8,128)(2,1)} %copy-done.6), channel_id=1, source_target_pairs={{0,128},{128,0},{1,129},{129,1},{2,130},{130,2},{3,131},{131,3},{4... | collective-permute-start | bytes 1769480 | tf_op jit(solution)/shard_map/ppermute | solution.py:307
  120.1 11.6 %collective-permute-start.35 = (bf16[2,128,384]{2,1,0:T(8,128)(2,1)S(1)}, bf16[2,128,384]{2,1,0:T(8,128)(2,1)S(1)}, u32[]{:S(2)}, u32[]{:S(2)}) collective-permute-start(bf16[2,128,384]{2,1,0:T(8,128)(2,1)S(1)} %get-tuple-element.95), channel_id=1, source_target_pairs={{0,1},{1,2},{2,3},{3,0},{4,5},{5,6},{6,7},{7,4},{8,9},{9,10},{10,1... | collective-permute-start | bytes 589832 | tf_op jit(solution)/shard_map/ppermute | solution.py:320
  121.0 10.7 %collective-permute-start.36 = (bf16[2,128,384]{2,1,0:T(8,128)(2,1)S(1)}, bf16[2,128,384]{2,1,0:T(8,128)(2,1)S(1)}, u32[]{:S(2)}, u32[]{:S(2)}) collective-permute-start(bf16[2,128,384]{2,1,0:T(8,128)(2,1)S(1)} %get-tuple-element.96), channel_id=1, source_target_pairs={{0,2},{1,3},{2,0},{3,1},{4,6},{5,7},{6,4},{7,5},{8,10},{9,11},{10,... | collective-permute-start | bytes 589832 | tf_op jit(solution)/shard_map/ppermute | solution.py:320
  123.1 9.1 %collective-permute-start.37 = (bf16[2,128,384]{2,1,0:T(8,128)(2,1)S(1)}, bf16[2,128,384]{2,1,0:T(8,128)(2,1)S(1)}, u32[]{:S(2)}, u32[]{:S(2)}) collective-permute-start(bf16[2,128,384]{2,1,0:T(8,128)(2,1)S(1)} %get-tuple-element.97), channel_id=1, source_target_pairs={{0,3},{1,0},{2,1},{3,2},{4,7},{5,4},{6,5},{7,6},{8,11},{9,8},{10,9... | collective-permute-start | bytes 589832 | tf_op jit(solution)/shard_map/ppermute | solution.py:320
  (30 other events, 176.6 us)
where the time goes:
time: 142 us; the launch traced here: 141 us
  waiting for transfers between devices  71.3 us (50%)
  starting transfers between devices  32.2 us (23%)
  Pallas kernels  15.3 us (11%)
  matrix products  10.6 us (7%)
  local copies, waits for them, and re-layouts  7.65 us (5%)
  other arithmetic  2.83 us (2%)
    ppermute x22, waiting for transfers between devices, along(): return lax.ppermute(value, ('z', 'core'), ring)  50.2 us
    ppermute x22, starting transfers between devices, along(): return lax.ppermute(value, ('z', 'core'), ring)  16 us
    dot_general x10, matrix products, dot(): return lax.dot_general(a, b, (over, ((), ())), preferred_element_type=F32)  10.6 us
    all_to_all x1, waiting for transfers between devices, shards(): lax.all_to_all(copies(tokens, ncol), ('xl', 'y'), 0, 0)  7.05 us
    ppermute x3, waiting for transfers between devices, shards(): lax.ppermute(for_y[hop], 'y', [(i, (i + hop) % ny) for i in range(ny)])  6.84 us
    pallas_call x2, Pallas kernels, scaled_sum(): pl.pallas_call(body, grid=(steps,), in_specs=[spec, spec, pl.BlockSpec((t...  5.96 us
    all_to_all x1, starting transfers between devices, shards(): lax.all_to_all(copies(tokens, ncol), ('xl', 'y'), 0, 0)  5.24 us
    ppermute x11, waiting for transfers between devices, swap(): return lax.ppermute(value, 'core', SWAP)  4.98 us
  transfers between devices with their start and end apart: 40, of which 30 were waited for; matrix products, arithmetic and copies ran while one was open for 12% of the time, Pallas kernels for 10%

commit v1 on v0

--- a/solution.py
+++ b/solution.py
@@ -50,20 +50,26 @@
 
 def activate(term, mine, theirs, cotangent, half, hidden=None):
     rows, cols = theirs.shape
-    steps = 3
+    steps = 1
     tile = cols // steps
     last = term.shape[0] // rows - 1
 
     def body(half, term, mine, theirs, cot, *refs):
         hidden, grad = refs[-2:]
-        v = term[...] + mine[...].astype(F32) + theirs[...].astype(F32)
-        sq = v * v
-        t = jnp.tanh(SQRT_2_PI * (v + 0.044715 * (sq * v)))
-        hidden[...] = (0.5 * v * (1.0 + t)).astype(BF16)
-        slope = 0.5 * (1.0 + t) + 0.5 * v * (1.0 - t * t) * (
-            SQRT_2_PI * (1.0 + 3 * 0.044715 * sq)
-        )
-        grad[...] = (cot[...].astype(F32) * slope).astype(BF16)
+
+        def rows_of(i, carry):
+            at = pl.ds(pl.multiple_of(i * 16, 16), 16)
+            v = term[at, :] + mine[at, :].astype(F32) + theirs[at, :].astype(F32)
+            sq = v * v
+            t = jnp.tanh(SQRT_2_PI * (v + 0.044715 * (sq * v)))
+            hidden[at, :] = (0.5 * v * (1.0 + t)).astype(BF16)
+            slope = 0.5 * (1.0 + t) + 0.5 * v * (1.0 - t * t) * (
+                SQRT_2_PI * (1.0 + 3 * 0.044715 * sq)
+            )
+            grad[at, :] = (cot[at, :].astype(F32) * slope).astype(BF16)
+            return carry
+
+        lax.fori_loop(0, rows // 16, rows_of, 0)
 
     near = pl.BlockSpec((rows, tile), lambda i, half: (0, i))
     wide = pl.BlockSpec((rows, tile), lambda i, half: (0, half[0] * steps + i))
@@ -142,12 +148,17 @@
 
 def scaled_sum(here, there, sent, scale, which, out=None):
     rows, cols = here.shape
-    steps = 3
+    steps = 1
     tile = rows // 2 // steps
 
     def body(here, there, sent, *refs):
-        total = here[...] + there[...].astype(F32) + sent[...].astype(F32)
-        refs[-1][...] = total * scale
+        def rows_of(i, carry):
+            at = pl.ds(pl.multiple_of(i * 16, 16), 16)
+            total = here[at, :] + there[at, :].astype(F32) + sent[at, :].astype(F32)
+            refs[-1][at, :] = total * scale
+            return carry
+
+        lax.fori_loop(0, tile // 16, rows_of, 0)
 
     spec = pl.BlockSpec((tile, cols), lambda i: (i + which * steps, 0))
     more = () if out is None else (out,)
@@ -320,7 +331,7 @@
         total += lax.ppermute(
             for_y[hop], "y", [(i, (i + hop) % ny) for i in range(ny)]
         ).astype(F32)
-    total = after(total.astype(BF16), sent[1], weight_grad)
+    total = after(total.astype(BF16), sent[1], own_terms)
     weight_grad = scaled_sum(*own_terms, sent[1], scale, 1, weight_grad)
     mine = place((y - z + nz) % ny) // ny == xl
     keep, send = jnp.where(mine, total[0], total[1]), jnp.where(mine, total[1], total[0])

time: 142 us -> 140 us (0.986)
  Pallas kernels: 15.3 us -> 13 us
  transfers between devices with their start and end apart: 40 -> 40, of which waited for: 30 -> 29; matrix products, arithmetic and copies ran while one was open for 12% -> 12% of each run, Pallas kernels for 10% -> 9%
where the time goes in v1:
time: 140 us; the launch traced here: 139 us
  waiting for transfers between devices  72.4 us (52%)
  starting transfers between devices  31.9 us (23%)
  Pallas kernels  13 us (9%)
  matrix products  10.5 us (8%)
  local copies, waits for them, and re-layouts  7.65 us (5%)
  other arithmetic  2.83 us (2%)
    ppermute x22, waiting for transfers between devices, along(): return lax.ppermute(value, ('z', 'core'), ring)  51.3 us
    ppermute x22, starting transfers between devices, along(): return lax.ppermute(value, ('z', 'core'), ring)  15.7 us
    dot_general x10, matrix products, dot(): return lax.dot_general(a, b, (over, ((), ())), preferred_element_type=F32)  10.5 us
    all_to_all x1, waiting for transfers between devices, shards(): lax.all_to_all(copies(tokens, ncol), ('xl', 'y'), 0, 0)  7.05 us
    ppermute x3, waiting for transfers between devices, shards(): lax.ppermute(for_y[hop], 'y', [(i, (i + hop) % ny) for i in range(ny)])  6.84 us
    all_to_all x1, starting transfers between devices, shards(): lax.all_to_all(copies(tokens, ncol), ('xl', 'y'), 0, 0)  5.24 us
    ppermute x11, waiting for transfers between devices, swap(): return lax.ppermute(value, 'core', SWAP)  5.13 us
    pallas_call x2, Pallas kernels, scaled_sum(): pl.pallas_call(body, grid=(steps,), in_specs=[spec, spec, pl.BlockSpec((t...  4.69 us
  transfers between devices with their start and end apart: 40, of which 29 were waited for; matrix products, arithmetic and copies ran while one was open for 12% of the time, Pallas kernels for 9%

profile of v1, /device:TPU:4, one launch (start us, length us, event | category | flops | bytes accessed | tf_op | source)
XLA Modules:
  0.0 139.5 jit_solution(16977759409177848087)
XLA Ops:
  2.6 5.2 %all-to-all-start = ((bf16[8,128,384]{2,1,0:T(8,128)(2,1)}), bf16[8,128,384]{2,1,0:T(8,128)(2,1)S(1)}, u32[]{:S(2)}, u32[]{:S(2)}) async-start(bf16[8,128,384]{2,1,0:T(8,128)(2,1)} %shard_map.58), calls=%async_computation | async-start | bytes 1572864 | tf_op jit(solution)/shard_map/all_to_all | solution.py:240
  13.4 7.1 %all-to-all-done = bf16[8,128,384]{2,1,0:T(8,128)(2,1)S(1)} async-done(((bf16[8,128,384]{2,1,0:T(8,128)(2,1)}), bf16[8,128,384]{2,1,0:T(8,128)(2,1)S(1)}, u32[]{:S(2)}, u32[]{:S(2)}) %all-to-all-start) | async-done | bytes 786464 | tf_op jit(solution)/shard_map/all_to_all | solution.py:240
  22.9 2.0 %collective-permute-start.7 = (bf16[64,1536]{1,0:T(8,128)(2,1)S(1)}, bf16[64,1536]{1,0:T(8,128)(2,1)S(1)}, u32[]{:S(2)}, u32[]{:S(2)}) collective-permute-start(bf16[64,1536]{1,0:T(8,128)(2,1)S(1)} %convolution_convert_fusion.2), channel_id=1, source_target_pairs={{0,16},{16,32},{32,48},{48,64},{64,80},{80,96},{96,112},{112,0},{8... | collective-permute-start | bytes 589832 | tf_op jit(solution)/shard_map/ppermute | solution.py:228
  27.2 2.0 %collective-permute-start.3 = (bf16[64,1536]{1,0:T(8,128)(2,1)S(1)}, bf16[64,1536]{1,0:T(8,128)(2,1)S(1)}, u32[]{:S(2)}, u32[]{:S(2)}) collective-permute-start(bf16[64,1536]{1,0:T(8,128)(2,1)S(1)} %convolution_convert_fusion.3), channel_id=1, source_target_pairs={{0,16},{16,32},{32,48},{48,64},{64,80},{80,96},{96,112},{112,0},{8... | collective-permute-start | bytes 589832 | tf_op jit(solution)/shard_map/ppermute | solution.py:228
  29.2 3.3 %collective-permute-done.7 = bf16[64,1536]{1,0:T(8,128)(2,1)S(1)} collective-permute-done((bf16[64,1536]{1,0:T(8,128)(2,1)S(1)}, bf16[64,1536]{1,0:T(8,128)(2,1)S(1)}, u32[]{:S(2)}, u32[]{:S(2)}) %collective-permute-start.7) | collective-permute-done | bytes 196640 | tf_op jit(solution)/shard_map/ppermute | solution.py:228
  35.8 5.9 %collective-permute-done.8 = bf16[128,1536]{1,0:T(8,128)(2,1)S(1)} collective-permute-done((bf16[128,1536]{1,0:T(8,128)(2,1)S(1)}, bf16[128,1536]{1,0:T(8,128)(2,1)S(1)}, u32[]{:S(2)}, u32[]{:S(2)}) %collective-permute-start.8) | collective-permute-done | bytes 393248 | tf_op jit(solution)/shard_map/ppermute | solution.py:228
  41.8 4.0 %collective-permute-done.4 = bf16[128,1536]{1,0:T(8,128)(2,1)S(1)} collective-permute-done((bf16[128,1536]{1,0:T(8,128)(2,1)S(1)}, bf16[128,1536]{1,0:T(8,128)(2,1)S(1)}, u32[]{:S(2)}, u32[]{:S(2)}) %collective-permute-start.4) | collective-permute-done | bytes 393248 | tf_op jit(solution)/shard_map/ppermute | solution.py:228
  46.0 4.8 %collective-permute-done.9 = bf16[128,1536]{1,0:T(8,128)(2,1)S(1)} collective-permute-done((bf16[128,1536]{1,0:T(8,128)(2,1)S(1)}, bf16[128,1536]{1,0:T(8,128)(2,1)S(1)}, u32[]{:S(2)}, u32[]{:S(2)}) %collective-permute-start.9) | collective-permute-done | bytes 393248 | tf_op jit(solution)/shard_map/ppermute | solution.py:228
  51.0 4.0 %collective-permute-done.5 = bf16[128,1536]{1,0:T(8,128)(2,1)S(1)} collective-permute-done((bf16[128,1536]{1,0:T(8,128)(2,1)S(1)}, bf16[128,1536]{1,0:T(8,128)(2,1)S(1)}, u32[]{:S(2)}, u32[]{:S(2)}) %collective-permute-start.5) | collective-permute-done | bytes 393248 | tf_op jit(solution)/shard_map/ppermute | solution.py:228
  55.2 4.8 %collective-permute-done.10.mine = bf16[128,1536]{1,0:T(8,128)(2,1)S(1)} collective-permute-done((bf16[128,1536]{1,0:T(8,128)(2,1)S(1)}, bf16[128,1536]{1,0:T(8,128)(2,1)S(1)}, u32[]{:S(2)}, u32[]{:S(2)}) %collective-permute-start.10) | collective-permute-done | bytes 393248 | tf_op jit(solution)/shard_map/ppermute | solution.py:228
  68.7 2.8 %collective-permute-done.21.refs_1_ = bf16[64,1536]{1,0:T(8,128)(2,1)S(1)} collective-permute-done((bf16[64,1536]{1,0:T(8,128)(2,1)S(1)}, bf16[64,1536]{1,0:T(8,128)(2,1)S(1)}, u32[]{:S(2)}, u32[]{:S(2)}) %collective-permute-start.21) | collective-permute-done | bytes 196640 | tf_op jit(solution)/shard_map/ppermute | solution.py:228
  74.0 2.0 %collective-permute-done.24.refs_3_ = bf16[64,1536]{1,0:T(8,128)(2,1)S(1)} collective-permute-done((bf16[64,1536]{1,0:T(8,128)(2,1)S(1)}, bf16[64,1536]{1,0:T(8,128)(2,1)S(1)}, u32[]{:S(2)}, u32[]{:S(2)}) %collective-permute-start.24) | collective-permute-done | bytes 196640 | tf_op jit(solution)/shard_map/ppermute | solution.py:228
  79.8 2.7 %collective-permute-done.14.refs_2_ = bf16[64,1536]{1,0:T(8,128)(2,1)S(1)} collective-permute-done((bf16[64,1536]{1,0:T(8,128)(2,1)S(1)}, bf16[64,1536]{1,0:T(8,128)(2,1)S(1)}, u32[]{:S(2)}, u32[]{:S(2)}) %collective-permute-start.14) | collective-permute-done | bytes 196640 | tf_op jit(solution)/shard_map/ppermute | solution.py:228
  84.4 2.4 %collective-permute-done.25.refs_4_ = bf16[64,1536]{1,0:T(8,128)(2,1)S(1)} collective-permute-done((bf16[64,1536]{1,0:T(8,128)(2,1)S(1)}, bf16[64,1536]{1,0:T(8,128)(2,1)S(1)}, u32[]{:S(2)}, u32[]{:S(2)}) %collective-permute-start.25) | collective-permute-done | bytes 196640 | tf_op jit(solution)/shard_map/ppermute | solution.py:228
  86.7 2.1 %collective-permute-start.28 = (bf16[64,1536]{1,0:T(8,128)(2,1)S(1)}, bf16[64,1536]{1,0:T(8,128)(2,1)S(1)}, u32[]{:S(2)}, u32[]{:S(2)}) collective-permute-start(bf16[64,1536]{1,0:T(8,128)(2,1)S(1)} %collective-permute-done.26.refs_5_), channel_id=1, source_target_pairs={{0,16},{16,32},{32,48},{48,64},{64,80},{80,96},{96,112},{112,0},{8... | collective-permute-start | bytes 589832 | tf_op jit(solution)/shard_map/ppermute | solution.py:228
  89.4 2.1 %collective-permute-done.18.refs_5_ = bf16[64,1536]{1,0:T(8,128)(2,1)S(1)} collective-permute-done((bf16[64,1536]{1,0:T(8,128)(2,1)S(1)}, bf16[64,1536]{1,0:T(8,128)(2,1)S(1)}, u32[]{:S(2)}, u32[]{:S(2)}) %collective-permute-start.18) | collective-permute-done | bytes 196640 | tf_op jit(solution)/shard_map/ppermute | solution.py:228
  91.5 2.1 %collective-permute-done.27.refs_6_ = bf16[64,1536]{1,0:T(8,128)(2,1)S(1)} collective-permute-done((bf16[64,1536]{1,0:T(8,128)(2,1)S(1)}, bf16[64,1536]{1,0:T(8,128)(2,1)S(1)}, u32[]{:S(2)}, u32[]{:S(2)}) %collective-permute-start.27) | collective-permute-done | bytes 196640 | tf_op jit(solution)/shard_map/ppermute | solution.py:228
  93.6 2.1 %collective-permute-done.28.refs_7_ = bf16[64,1536]{1,0:T(8,128)(2,1)S(1)} collective-permute-done((bf16[64,1536]{1,0:T(8,128)(2,1)S(1)}, bf16[64,1536]{1,0:T(8,128)(2,1)S(1)}, u32[]{:S(2)}, u32[]{:S(2)}) %collective-permute-start.28) | collective-permute-done | bytes 196640 | tf_op jit(solution)/shard_map/ppermute | solution.py:228
  104.3 2.1 %collective-permute-done.20.refs_7_ = bf16[64,1536]{1,0:T(8,128)(2,1)S(1)} collective-permute-done((bf16[64,1536]{1,0:T(8,128)(2,1)S(1)}, bf16[64,1536]{1,0:T(8,128)(2,1)S(1)}, u32[]{:S(2)}, u32[]{:S(2)}) %collective-permute-start.20) | collective-permute-done | bytes 196640 | tf_op jit(solution)/shard_map/ppermute | solution.py:228
  116.9 2.1 %collective-permute-done.33.sent = bf16[192,1536]{1,0:T(8,128)(2,1)} collective-permute-done((bf16[192,1536]{1,0:T(8,128)(2,1)}, bf16[192,1536]{1,0:T(8,128)(2,1)}, u32[]{:S(2)}, u32[]{:S(2)}) %collective-permute-start.33) | collective-permute-done | bytes 589856 | tf_op jit(solution)/shard_map/ppermute | solution.py:318
  121.1 2.1 %collective-permute-start.36 = (bf16[2,128,384]{2,1,0:T(8,128)(2,1)S(1)}, bf16[2,128,384]{2,1,0:T(8,128)(2,1)S(1)}, u32[]{:S(2)}, u32[]{:S(2)}) collective-permute-start(bf16[2,128,384]{2,1,0:T(8,128)(2,1)S(1)} %get-tuple-element.96), channel_id=1, source_target_pairs={{0,2},{1,3},{2,0},{3,1},{4,6},{5,7},{6,4},{7,5},{8,10},{9,11},{10,... | collective-permute-start | bytes 589832 | tf_op jit(solution)/shard_map/ppermute | solution.py:331
  125.5 6.3 %collective-permute-done.35 = bf16[2,128,384]{2,1,0:T(8,128)(2,1)S(1)} collective-permute-done((bf16[2,128,384]{2,1,0:T(8,128)(2,1)S(1)}, bf16[2,128,384]{2,1,0:T(8,128)(2,1)S(1)}, u32[]{:S(2)}, u32[]{:S(2)}) %collective-permute-start.35) | collective-permute-done | bytes 196640 | tf_op jit(solution)/shard_map/ppermute | solution.py:331
  134.1 2.3 %shard_map.67.refs_0_ = f32[384,1536]{1,0:T(8,128)} custom-call(f32[384,1536]{1,0:T(8,128)S(1)} %fusion.12.here, bf16[384,1536]{1,0:T(8,128)(2,1)S(1)} %collective-permute-done.31.there, bf16[192,1536]{1,0:T(8,128)(2,1)} %collective-permute-done.33.sent), custom_call_target="tpu_custom_call" | custom-call | flops 1 | bytes 1 | tf_op jit(solution)/shard_map/pallas_call | solution.py:165
  136.4 2.3 %shard_map.68 = f32[384,1536]{1,0:T(8,128)} custom-call(f32[384,1536]{1,0:T(8,128)S(1)} %fusion.12.here, bf16[384,1536]{1,0:T(8,128)(2,1)S(1)} %collective-permute-done.31.there, bf16[192,1536]{1,0:T(8,128)(2,1)} %collective-permute-done.32.sent, f32[384,1536]{1,0:T(8,128)} %shard_map.67.refs_0_), custom_call_target="tpu_custom_call", output_to_operand_aliasing={{}: (3, {})} | custom-call | flops 1 | bytes 1 | tf_op jit(solution)/shard_map/pallas_call | solution.py:165
  (128 shorter events, 59.8 us)
Async XLA Ops:
  0.6 8.9 %collective-permute-start = (bf16[384,3072]{1,0:T(8,128)(2,1)}, bf16[384,3072]{1,0:T(8,128)(2,1)}, u32[]{:S(2)}, u32[]{:S(2)}) collective-permute-start(bf16[384,3072]{1,0:T(8,128)(2,1)} %param.4), channel_id=1, source_target_pairs={{0,8},{8,0},{1,9},{9,1},{2,10},{10,2},{3,11},{11,3},{4,12},{12,4},... | collective-permute-start | bytes 7077896 | tf_op jit(solution)/shard_map/ppermute | solution.py:225
  2.6 17.9 %all-to-all-start = ((bf16[8,128,384]{2,1,0:T(8,128)(2,1)}), bf16[8,128,384]{2,1,0:T(8,128)(2,1)S(1)}, u32[]{:S(2)}, u32[]{:S(2)}) async-start(bf16[8,128,384]{2,1,0:T(8,128)(2,1)} %shard_map.58), calls=%async_computation | async-start | bytes 1572864 | tf_op jit(solution)/shard_map/all_to_all | solution.py:240
  22.9 9.6 %collective-permute-start.7 = (bf16[64,1536]{1,0:T(8,128)(2,1)S(1)}, bf16[64,1536]{1,0:T(8,128)(2,1)S(1)}, u32[]{:S(2)}, u32[]{:S(2)}) collective-permute-start(bf16[64,1536]{1,0:T(8,128)(2,1)S(1)} %convolution_convert_fusion.2), channel_id=1, source_target_pairs={{0,16},{16,32},{32,48},{48,64},{64,80},{80,96},{96,112},{112,0},{8... | collective-permute-start | bytes 589832 | tf_op jit(solution)/shard_map/ppermute | solution.py:228
  32.6 9.1 %collective-permute-start.8 = (bf16[128,1536]{1,0:T(8,128)(2,1)S(1)}, bf16[128,1536]{1,0:T(8,128)(2,1)S(1)}, u32[]{:S(2)}, u32[]{:S(2)}) collective-permute-start(bf16[128,1536]{1,0:T(8,128)(2,1)S(1)} %fusion), channel_id=1, source_target_pairs={{0,16},{16,32},{32,48},{48,64},{64,80},{80,96},{96,112},{112,0},{8... | collective-permute-start | bytes 1179656 | tf_op jit(solution)/shard_map/ppermute | solution.py:228
  35.0 10.9 %collective-permute-start.4 = (bf16[128,1536]{1,0:T(8,128)(2,1)S(1)}, bf16[128,1536]{1,0:T(8,128)(2,1)S(1)}, u32[]{:S(2)}, u32[]{:S(2)}) collective-permute-start(bf16[128,1536]{1,0:T(8,128)(2,1)S(1)} %fusion.3), channel_id=1, source_target_pairs={{0,16},{16,32},{32,48},{48,64},{64,80},{80,96},{96,112},{112,0},{8... | collective-permute-start | bytes 1179656 | tf_op jit(solution)/shard_map/ppermute | solution.py:228
  41.7 9.1 %collective-permute-start.9 = (bf16[128,1536]{1,0:T(8,128)(2,1)S(1)}, bf16[128,1536]{1,0:T(8,128)(2,1)S(1)}, u32[]{:S(2)}, u32[]{:S(2)}) collective-permute-start(bf16[128,1536]{1,0:T(8,128)(2,1)S(1)} %fusion.1), channel_id=1, source_target_pairs={{0,16},{16,32},{32,48},{48,64},{64,80},{80,96},{96,112},{112,0},{8... | collective-permute-start | bytes 1179656 | tf_op jit(solution)/shard_map/ppermute | solution.py:228
  45.9 9.1 %collective-permute-start.5 = (bf16[128,1536]{1,0:T(8,128)(2,1)S(1)}, bf16[128,1536]{1,0:T(8,128)(2,1)S(1)}, u32[]{:S(2)}, u32[]{:S(2)}) collective-permute-start(bf16[128,1536]{1,0:T(8,128)(2,1)S(1)} %fusion.4), channel_id=1, source_target_pairs={{0,16},{16,32},{32,48},{48,64},{64,80},{80,96},{96,112},{112,0},{8... | collective-permute-start | bytes 1179656 | tf_op jit(solution)/shard_map/ppermute | solution.py:228
  50.9 9.1 %collective-permute-start.10 = (bf16[128,1536]{1,0:T(8,128)(2,1)S(1)}, bf16[128,1536]{1,0:T(8,128)(2,1)S(1)}, u32[]{:S(2)}, u32[]{:S(2)}) collective-permute-start(bf16[128,1536]{1,0:T(8,128)(2,1)S(1)} %fusion.2), channel_id=1, source_target_pairs={{0,16},{16,32},{32,48},{48,64},{64,80},{80,96},{96,112},{112,0},{8... | collective-permute-start | bytes 1179656 | tf_op jit(solution)/shard_map/ppermute | solution.py:228
  55.1 9.1 %collective-permute-start.6 = (bf16[128,1536]{1,0:T(8,128)(2,1)S(1)}, bf16[128,1536]{1,0:T(8,128)(2,1)S(1)}, u32[]{:S(2)}, u32[]{:S(2)}) collective-permute-start(bf16[128,1536]{1,0:T(8,128)(2,1)S(1)} %fusion.5), channel_id=1, source_target_pairs={{0,16},{16,32},{32,48},{48,64},{64,80},{80,96},{96,112},{112,0},{8... | collective-permute-start | bytes 1179656 | tf_op jit(solution)/shard_map/ppermute | solution.py:228
  67.8 8.3 %collective-permute-start.24 = (bf16[64,1536]{1,0:T(8,128)(2,1)S(1)}, bf16[64,1536]{1,0:T(8,128)(2,1)S(1)}, u32[]{:S(2)}, u32[]{:S(2)}) collective-permute-start(bf16[64,1536]{1,0:T(8,128)(2,1)S(1)} %collective-permute-done.23), channel_id=1, source_target_pairs={{0,16},{16,32},{32,48},{48,64},{64,80},{80,96},{96,112},{112,0},{8... | collective-permute-start | bytes 589832 | tf_op jit(solution)/shard_map/ppermute | solution.py:228
  72.4 10.2 %collective-permute-start.16 = (bf16[64,1536]{1,0:T(8,128)(2,1)S(1)}, bf16[64,1536]{1,0:T(8,128)(2,1)S(1)}, u32[]{:S(2)}, u32[]{:S(2)}) collective-permute-start(bf16[64,1536]{1,0:T(8,128)(2,1)S(1)} %collective-permute-done.15), channel_id=1, source_target_pairs={{0,16},{16,32},{32,48},{48,64},{64,80},{80,96},{96,112},{112,0},{8... | collective-permute-start | bytes 589832 | tf_op jit(solution)/shard_map/ppermute | solution.py:228
  73.9 8.6 %collective-permute-start.14 = (bf16[64,1536]{1,0:T(8,128)(2,1)S(1)}, bf16[64,1536]{1,0:T(8,128)(2,1)S(1)}, u32[]{:S(2)}, u32[]{:S(2)}) collective-permute-start(bf16[64,1536]{1,0:T(8,128)(2,1)S(1)} %collective-permute-done.13.refs_1_), channel_id=1, source_target_pairs={{0,16},{16,32},{32,48},{48,64},{64,80},{80,96},{96,112},{112,0},{8... | collective-permute-start | bytes 589832 | tf_op jit(solution)/shard_map/ppermute | solution.py:228
  76.1 10.7 %collective-permute-start.26 = (bf16[64,1536]{1,0:T(8,128)(2,1)S(1)}, bf16[64,1536]{1,0:T(8,128)(2,1)S(1)}, u32[]{:S(2)}, u32[]{:S(2)}) collective-permute-start(bf16[64,1536]{1,0:T(8,128)(2,1)S(1)} %collective-permute-done.24.refs_3_), channel_id=1, source_target_pairs={{0,16},{16,32},{32,48},{48,64},{64,80},{80,96},{96,112},{112,0},{8... | collective-permute-start | bytes 589832 | tf_op jit(solution)/shard_map/ppermute | solution.py:228
  78.3 8.4 %collective-permute-start.25 = (bf16[64,1536]{1,0:T(8,128)(2,1)S(1)}, bf16[64,1536]{1,0:T(8,128)(2,1)S(1)}, u32[]{:S(2)}, u32[]{:S(2)}) collective-permute-start(bf16[64,1536]{1,0:T(8,128)(2,1)S(1)} %collective-permute-done.22.refs_2_), channel_id=1, source_target_pairs={{0,16},{16,32},{32,48},{48,64},{64,80},{80,96},{96,112},{112,0},{8... | collective-permute-start | bytes 589832 | tf_op jit(solution)/shard_map/ppermute | solution.py:228
  79.0 17.1 %collective-permute-start.29 = (bf16[512,384]{1,0:T(8,128)(2,1)S(1)}, bf16[512,384]{1,0:T(8,128)(2,1)S(1)}, u32[]{:S(2)}, u32[]{:S(2)}) collective-permute-start(bf16[512,384]{1,0:T(8,128)(2,1)S(1)} %get-tuple-element.73), channel_id=1, source_target_pairs={{0,8},{8,0},{1,9},{9,1},{2,10},{10,2},{3,11},{11,3},{4,12},{12,4},... | collective-permute-start | bytes 1179656 | tf_op jit(solution)/shard_map/ppermute | solution.py:225
  82.5 9.0 %collective-permute-start.18 = (bf16[64,1536]{1,0:T(8,128)(2,1)S(1)}, bf16[64,1536]{1,0:T(8,128)(2,1)S(1)}, u32[]{:S(2)}, u32[]{:S(2)}) collective-permute-start(bf16[64,1536]{1,0:T(8,128)(2,1)S(1)} %collective-permute-done.16.refs_3_), channel_id=1, source_target_pairs={{0,16},{16,32},{32,48},{48,64},{64,80},{80,96},{96,112},{112,0},{8... | collective-permute-start | bytes 589832 | tf_op jit(solution)/shard_map/ppermute | solution.py:228
  86.7 9.0 %collective-permute-start.28 = (bf16[64,1536]{1,0:T(8,128)(2,1)S(1)}, bf16[64,1536]{1,0:T(8,128)(2,1)S(1)}, u32[]{:S(2)}, u32[]{:S(2)}) collective-permute-start(bf16[64,1536]{1,0:T(8,128)(2,1)S(1)} %collective-permute-done.26.refs_5_), channel_id=1, source_target_pairs={{0,16},{16,32},{32,48},{48,64},{64,80},{80,96},{96,112},{112,0},{8... | collective-permute-start | bytes 589832 | tf_op jit(solution)/shard_map/ppermute | solution.py:228
  97.4 9.0 %collective-permute-start.20 = (bf16[64,1536]{1,0:T(8,128)(2,1)S(1)}, bf16[64,1536]{1,0:T(8,128)(2,1)S(1)}, u32[]{:S(2)}, u32[]{:S(2)}) collective-permute-start(bf16[64,1536]{1,0:T(8,128)(2,1)S(1)} %collective-permute-done.18.refs_5_), channel_id=1, source_target_pairs={{0,16},{16,32},{32,48},{48,64},{64,80},{80,96},{96,112},{112,0},{8... | collective-permute-start | bytes 589832 | tf_op jit(solution)/shard_map/ppermute | solution.py:228
  101.8 17.2 %collective-permute-start.33 = (bf16[192,1536]{1,0:T(8,128)(2,1)}, bf16[192,1536]{1,0:T(8,128)(2,1)}, u32[]{:S(2)}, u32[]{:S(2)}) collective-permute-start(bf16[192,1536]{1,0:T(8,128)(2,1)} %get-tuple-element.74), channel_id=1, source_target_pairs={{0,128},{128,0},{1,129},{129,1},{2,130},{130,2},{3,131},{131,3},{4... | collective-permute-start | bytes 1769480 | tf_op jit(solution)/shard_map/ppermute | solution.py:318
  113.1 19.3 %collective-permute-start.31 = (bf16[384,1536]{1,0:T(8,128)(2,1)}, bf16[384,1536]{1,0:T(8,128)(2,1)S(1)}, u32[]{:S(2)}, u32[]{:S(2)}) collective-permute-start(bf16[384,1536]{1,0:T(8,128)(2,1)} %convolution_convert_fusion), channel_id=1, source_target_pairs={{0,8},{8,0},{1,9},{9,1},{2,10},{10,2},{3,11},{11,3},{4,12},{12,4},... | collective-permute-start | bytes 3538952 | tf_op jit(solution)/shard_map/ppermute | solution.py:225
  114.5 17.9 %collective-permute-start.32 = (bf16[192,1536]{1,0:T(8,128)(2,1)}, bf16[192,1536]{1,0:T(8,128)(2,1)}, u32[]{:S(2)}, u32[]{:S(2)}) collective-permute-start(bf16[192,1536]{1,0:T(8,128)(2,1)} %copy-done.6), channel_id=1, source_target_pairs={{0,128},{128,0},{1,129},{129,1},{2,130},{130,2},{3,131},{131,3},{4... | collective-permute-start | bytes 1769480 | tf_op jit(solution)/shard_map/ppermute | solution.py:318
  120.1 11.6 %collective-permute-start.35 = (bf16[2,128,384]{2,1,0:T(8,128)(2,1)S(1)}, bf16[2,128,384]{2,1,0:T(8,128)(2,1)S(1)}, u32[]{:S(2)}, u32[]{:S(2)}) collective-permute-start(bf16[2,128,384]{2,1,0:T(8,128)(2,1)S(1)} %get-tuple-element.95), channel_id=1, source_target_pairs={{0,1},{1,2},{2,3},{3,0},{4,5},{5,6},{6,7},{7,4},{8,9},{9,10},{10,1... | collective-permute-start | bytes 589832 | tf_op jit(solution)/shard_map/ppermute | solution.py:331
  121.1 10.7 %collective-permute-start.36 = (bf16[2,128,384]{2,1,0:T(8,128)(2,1)S(1)}, bf16[2,128,384]{2,1,0:T(8,128)(2,1)S(1)}, u32[]{:S(2)}, u32[]{:S(2)}) collective-permute-start(bf16[2,128,384]{2,1,0:T(8,128)(2,1)S(1)} %get-tuple-element.96), channel_id=1, source_target_pairs={{0,2},{1,3},{2,0},{3,1},{4,6},{5,7},{6,4},{7,5},{8,10},{9,11},{10,... | collective-permute-start | bytes 589832 | tf_op jit(solution)/shard_map/ppermute | solution.py:331
  123.2 9.1 %collective-permute-start.37 = (bf16[2,128,384]{2,1,0:T(8,128)(2,1)S(1)}, bf16[2,128,384]{2,1,0:T(8,128)(2,1)S(1)}, u32[]{:S(2)}, u32[]{:S(2)}) collective-permute-start(bf16[2,128,384]{2,1,0:T(8,128)(2,1)S(1)} %get-tuple-element.97), channel_id=1, source_target_pairs={{0,3},{1,0},{2,1},{3,2},{4,7},{5,4},{6,5},{7,6},{8,11},{9,8},{10,9... | collective-permute-start | bytes 589832 | tf_op jit(solution)/shard_map/ppermute | solution.py:331
  (30 other events, 178.2 us)

commit v2 on v1

--- a/solution.py
+++ b/solution.py
@@ -130,7 +130,7 @@
     tile = cols // steps
 
     def body(here, there, *outs):
-        total = (here[...] + there[...].astype(F32)).astype(BF16)
+        total = (here[...].astype(F32) + there[...].astype(F32)).astype(BF16)
         outs[0][...] = total[: rows // 2]
         outs[1][...] = total[rows // 2 :]
 
@@ -146,32 +146,34 @@
     )(here, there)
 
 
-def scaled_sum(here, there, sent, scale, which, out=None):
+def scaled_sum(here, there, sent, scale):
     rows, cols = here.shape
-    steps = 1
-    tile = rows // 2 // steps
-
-    def body(here, there, sent, *refs):
-        def rows_of(i, carry):
-            at = pl.ds(pl.multiple_of(i * 16, 16), 16)
-            total = here[at, :] + there[at, :].astype(F32) + sent[at, :].astype(F32)
-            refs[-1][at, :] = total * scale
-            return carry
-
-        lax.fori_loop(0, tile // 16, rows_of, 0)
-
-    spec = pl.BlockSpec((tile, cols), lambda i: (i + which * steps, 0))
-    more = () if out is None else (out,)
-    return pl.pallas_call(
-        body,
-        grid=(steps,),
-        in_specs=[spec, spec, pl.BlockSpec((tile, cols), lambda i: (i, 0))]
-        + [pl.BlockSpec(memory_space=pl.ANY)] * len(more),
+    half = rows // 2
+
+    def body(here, there, *refs):
+        sent, out = refs[:-1], refs[-1]
+
+        def add(sent):
+            def rows_of(i, carry):
+                at = pl.ds(pl.multiple_of(i * 16, 16), 16)
+                total = here[at, :].astype(F32) + there[at, :].astype(F32) + sent[at, :].astype(F32)
+                out[at, :] = total * scale
+                return carry
+
+            lax.fori_loop(0, half // 16, rows_of, 0)
+
+        for k, ref in enumerate(sent):
+            pl.when(pl.program_id(0) == k)(lambda ref=ref: add(ref))
+
+    spec = pl.BlockSpec((half, cols), lambda i: (i, 0))
+    return pl.pallas_call(
+        body,
+        grid=(2,),
+        in_specs=[spec, spec] + [pl.BlockSpec((half, cols), lambda i: (0, 0))] * 2,
         out_specs=spec,
         out_shape=jax.ShapeDtypeStruct((rows, cols), F32),
-        input_output_aliases={} if out is None else {3: 0},
-        **PARAMS,
-    )(here, there, sent, *more)
+        **PARAMS,
+    )(here, there, *sent)
 
 
 def by_y(here, there, scalars, rows, ny):
@@ -312,7 +314,7 @@
 
     def weight_terms(block):
         there = swap(dot(x_back[:, depth:], block, BY_ROWS).astype(BF16))
-        return dot(x_back[:, :depth], block, BY_ROWS), there
+        return dot(x_back[:, :depth], block, BY_ROWS).astype(BF16), there
 
     to_peer = rounded_sum(*weight_terms(stacked(blocks[0])))
     sent = [lax.ppermute(p, "dp", SWAP) for p in to_peer]
@@ -325,14 +327,13 @@
     for_y = by_y(here, there, scalars, rows, ny)
     own_terms = weight_terms(after(blocks[1], out))
     scale = float(nz * rows * lax.axis_size("dp")) ** (-0.5)
-    weight_grad = scaled_sum(*own_terms, sent[0], scale, 0)
     total = for_y[0].astype(F32)
     for hop in range(1, ny):
         total += lax.ppermute(
             for_y[hop], "y", [(i, (i + hop) % ny) for i in range(ny)]
         ).astype(F32)
     total = after(total.astype(BF16), sent[1], own_terms)
-    weight_grad = scaled_sum(*own_terms, sent[1], scale, 1, weight_grad)
+    weight_grad = scaled_sum(*own_terms, sent, scale)
     mine = place((y - z + nz) % ny) // ny == xl
     keep, send = jnp.where(mine, total[0], total[1]), jnp.where(mine, total[1], total[0])
     input_grad = (

time: 140 us -> 138 us (0.986)
  Pallas kernels: 13 us -> 10.8 us
    pallas_call x2 -> x1, Pallas kernels: 4.69 us -> 2.95 us  [scaled_sum(): pl.pallas_call(body, grid=(2,), in_specs=[spec, spec] + [pl.BlockSpec((ha...]
    unnamed x30 -> x24, local copies, waits for them, and re-layouts: 2.97 us -> 2.97 us
  transfers between devices with their start and end apart: 40 -> 40, of which waited for: 29 -> 30; matrix products, arithmetic and copies ran while one was open for 12% -> 13% of each run, Pallas kernels for 9% -> 7%
where the time goes in v2:
time: 138 us; the launch traced here: 137 us
  waiting for transfers between devices  71.6 us (52%)
  starting transfers between devices  31.9 us (23%)
  matrix products  11.5 us (8%)
  Pallas kernels  10.8 us (8%)
  local copies, waits for them, and re-layouts  7.61 us (6%)
  other arithmetic  2.83 us (2%)
    ppermute x22, waiting for transfers between devices, along(): return lax.ppermute(value, ('z', 'core'), ring)  51.3 us
    ppermute x22, starting transfers between devices, along(): return lax.ppermute(value, ('z', 'core'), ring)  15.7 us
    dot_general x10, matrix products, dot(): return lax.dot_general(a, b, (over, ((), ())), preferred_element_type=F32)  11.5 us
    all_to_all x1, waiting for transfers between devices, shards(): lax.all_to_all(copies(tokens, ncol), ('xl', 'y'), 0, 0)  7.05 us
    ppermute x3, waiting for transfers between devices, shards(): lax.ppermute(for_y[hop], 'y', [(i, (i + hop) % ny) for i in range(ny)])  5.84 us
    all_to_all x1, starting transfers between devices, shards(): lax.all_to_all(copies(tokens, ncol), ('xl', 'y'), 0, 0)  5.24 us
    ppermute x11, waiting for transfers between devices, swap(): return lax.ppermute(value, 'core', SWAP)  5.03 us
    ppermute x3, starting transfers between devices, shards(): lax.ppermute(for_y[hop], 'y', [(i, (i + hop) % ny) for i in range(ny)])  4.56 us
  transfers between devices with their start and end apart: 40, of which 30 were waited for; matrix products, arithmetic and copies ran while one was open for 13% of the time, Pallas kernels for 7%

profile of v2, /device:TPU:4, one launch (start us, length us, event | category | flops | bytes accessed | tf_op | source)
XLA Modules:
  0.0 137.4 jit_solution(5872395689859239604)
XLA Ops:
  2.6 5.2 %all-to-all-start = ((bf16[8,128,384]{2,1,0:T(8,128)(2,1)}), bf16[8,128,384]{2,1,0:T(8,128)(2,1)S(1)}, u32[]{:S(2)}, u32[]{:S(2)}) async-start(bf16[8,128,384]{2,1,0:T(8,128)(2,1)} %shard_map.58), calls=%async_computation | async-start | bytes 1572864 | tf_op jit(solution)/shard_map/all_to_all | solution.py:242
  9.6 1.9 %constant_dynamic-slice_fusion = (bf16[384,1536]{1,0:T(8,128)(2,1)S(1)}, bf16[384,1536]{1,0:T(8,128)(2,1)S(1)}) fusion(bf16[384,3072]{1,0:T(8,128)(2,1)} %collective-permute-done, s32[]{:T(128)S(6)} %select_n.123, s32[]{:T(128)S(6)} %select_n.122), kind=kLoop, calls=%fused_computation.29 | loop fusion | bytes 4718600 | tf_op jit(solution)/shard_map/dynamic_slice | solution.py:22
  13.4 7.1 %all-to-all-done = bf16[8,128,384]{2,1,0:T(8,128)(2,1)S(1)} async-done(((bf16[8,128,384]{2,1,0:T(8,128)(2,1)}), bf16[8,128,384]{2,1,0:T(8,128)(2,1)S(1)}, u32[]{:S(2)}, u32[]{:S(2)}) %all-to-all-start) | async-done | bytes 786464 | tf_op jit(solution)/shard_map/all_to_all | solution.py:242
  23.0 2.0 %collective-permute-start.7 = (bf16[64,1536]{1,0:T(8,128)(2,1)S(1)}, bf16[64,1536]{1,0:T(8,128)(2,1)S(1)}, u32[]{:S(2)}, u32[]{:S(2)}) collective-permute-start(bf16[64,1536]{1,0:T(8,128)(2,1)S(1)} %convolution_convert_fusion.4), channel_id=1, source_target_pairs={{0,16},{16,32},{32,48},{48,64},{64,80},{80,96},{96,112},{112,0},{8... | collective-permute-start | bytes 589832 | tf_op jit(solution)/shard_map/ppermute | solution.py:230
  27.2 2.0 %collective-permute-start.3 = (bf16[64,1536]{1,0:T(8,128)(2,1)S(1)}, bf16[64,1536]{1,0:T(8,128)(2,1)S(1)}, u32[]{:S(2)}, u32[]{:S(2)}) collective-permute-start(bf16[64,1536]{1,0:T(8,128)(2,1)S(1)} %convolution_convert_fusion.5), channel_id=1, source_target_pairs={{0,16},{16,32},{32,48},{48,64},{64,80},{80,96},{96,112},{112,0},{8... | collective-permute-start | bytes 589832 | tf_op jit(solution)/shard_map/ppermute | solution.py:230
  29.2 3.3 %collective-permute-done.7 = bf16[64,1536]{1,0:T(8,128)(2,1)S(1)} collective-permute-done((bf16[64,1536]{1,0:T(8,128)(2,1)S(1)}, bf16[64,1536]{1,0:T(8,128)(2,1)S(1)}, u32[]{:S(2)}, u32[]{:S(2)}) %collective-permute-start.7) | collective-permute-done | bytes 196640 | tf_op jit(solution)/shard_map/ppermute | solution.py:230
  35.8 5.9 %collective-permute-done.8 = bf16[128,1536]{1,0:T(8,128)(2,1)S(1)} collective-permute-done((bf16[128,1536]{1,0:T(8,128)(2,1)S(1)}, bf16[128,1536]{1,0:T(8,128)(2,1)S(1)}, u32[]{:S(2)}, u32[]{:S(2)}) %collective-permute-start.8) | collective-permute-done | bytes 393248 | tf_op jit(solution)/shard_map/ppermute | solution.py:230
  41.9 4.0 %collective-permute-done.4 = bf16[128,1536]{1,0:T(8,128)(2,1)S(1)} collective-permute-done((bf16[128,1536]{1,0:T(8,128)(2,1)S(1)}, bf16[128,1536]{1,0:T(8,128)(2,1)S(1)}, u32[]{:S(2)}, u32[]{:S(2)}) %collective-permute-start.4) | collective-permute-done | bytes 393248 | tf_op jit(solution)/shard_map/ppermute | solution.py:230
  46.0 4.8 %collective-permute-done.9 = bf16[128,1536]{1,0:T(8,128)(2,1)S(1)} collective-permute-done((bf16[128,1536]{1,0:T(8,128)(2,1)S(1)}, bf16[128,1536]{1,0:T(8,128)(2,1)S(1)}, u32[]{:S(2)}, u32[]{:S(2)}) %collective-permute-start.9) | collective-permute-done | bytes 393248 | tf_op jit(solution)/shard_map/ppermute | solution.py:230
  51.0 4.0 %collective-permute-done.5 = bf16[128,1536]{1,0:T(8,128)(2,1)S(1)} collective-permute-done((bf16[128,1536]{1,0:T(8,128)(2,1)S(1)}, bf16[128,1536]{1,0:T(8,128)(2,1)S(1)}, u32[]{:S(2)}, u32[]{:S(2)}) %collective-permute-start.5) | collective-permute-done | bytes 393248 | tf_op jit(solution)/shard_map/ppermute | solution.py:230
  55.2 4.8 %collective-permute-done.10.mine = bf16[128,1536]{1,0:T(8,128)(2,1)S(1)} collective-permute-done((bf16[128,1536]{1,0:T(8,128)(2,1)S(1)}, bf16[128,1536]{1,0:T(8,128)(2,1)S(1)}, u32[]{:S(2)}, u32[]{:S(2)}) %collective-permute-start.10) | collective-permute-done | bytes 393248 | tf_op jit(solution)/shard_map/ppermute | solution.py:230
  68.7 2.8 %collective-permute-done.21.refs_1_ = bf16[64,1536]{1,0:T(8,128)(2,1)S(1)} collective-permute-done((bf16[64,1536]{1,0:T(8,128)(2,1)S(1)}, bf16[64,1536]{1,0:T(8,128)(2,1)S(1)}, u32[]{:S(2)}, u32[]{:S(2)}) %collective-permute-start.21) | collective-permute-done | bytes 196640 | tf_op jit(solution)/shard_map/ppermute | solution.py:230
  74.0 2.0 %collective-permute-done.24.refs_3_ = bf16[64,1536]{1,0:T(8,128)(2,1)S(1)} collective-permute-done((bf16[64,1536]{1,0:T(8,128)(2,1)S(1)}, bf16[64,1536]{1,0:T(8,128)(2,1)S(1)}, u32[]{:S(2)}, u32[]{:S(2)}) %collective-permute-start.24) | collective-permute-done | bytes 196640 | tf_op jit(solution)/shard_map/ppermute | solution.py:230
  79.8 2.7 %collective-permute-done.14.refs_2_ = bf16[64,1536]{1,0:T(8,128)(2,1)S(1)} collective-permute-done((bf16[64,1536]{1,0:T(8,128)(2,1)S(1)}, bf16[64,1536]{1,0:T(8,128)(2,1)S(1)}, u32[]{:S(2)}, u32[]{:S(2)}) %collective-permute-start.14) | collective-permute-done | bytes 196640 | tf_op jit(solution)/shard_map/ppermute | solution.py:230
  84.4 2.4 %collective-permute-done.25.refs_4_ = bf16[64,1536]{1,0:T(8,128)(2,1)S(1)} collective-permute-done((bf16[64,1536]{1,0:T(8,128)(2,1)S(1)}, bf16[64,1536]{1,0:T(8,128)(2,1)S(1)}, u32[]{:S(2)}, u32[]{:S(2)}) %collective-permute-start.25) | collective-permute-done | bytes 196640 | tf_op jit(solution)/shard_map/ppermute | solution.py:230
  86.8 2.1 %collective-permute-start.28 = (bf16[64,1536]{1,0:T(8,128)(2,1)S(1)}, bf16[64,1536]{1,0:T(8,128)(2,1)S(1)}, u32[]{:S(2)}, u32[]{:S(2)}) collective-permute-start(bf16[64,1536]{1,0:T(8,128)(2,1)S(1)} %collective-permute-done.26.refs_5_), channel_id=1, source_target_pairs={{0,16},{16,32},{32,48},{48,64},{64,80},{80,96},{96,112},{112,0},{8... | collective-permute-start | bytes 589832 | tf_op jit(solution)/shard_map/ppermute | solution.py:230
  89.4 2.1 %collective-permute-done.18.refs_5_ = bf16[64,1536]{1,0:T(8,128)(2,1)S(1)} collective-permute-done((bf16[64,1536]{1,0:T(8,128)(2,1)S(1)}, bf16[64,1536]{1,0:T(8,128)(2,1)S(1)}, u32[]{:S(2)}, u32[]{:S(2)}) %collective-permute-start.18) | collective-permute-done | bytes 196640 | tf_op jit(solution)/shard_map/ppermute | solution.py:230
  91.5 2.1 %collective-permute-done.27.refs_6_ = bf16[64,1536]{1,0:T(8,128)(2,1)S(1)} collective-permute-done((bf16[64,1536]{1,0:T(8,128)(2,1)S(1)}, bf16[64,1536]{1,0:T(8,128)(2,1)S(1)}, u32[]{:S(2)}, u32[]{:S(2)}) %collective-permute-start.27) | collective-permute-done | bytes 196640 | tf_op jit(solution)/shard_map/ppermute | solution.py:230
  93.6 2.1 %collective-permute-done.28.refs_7_ = bf16[64,1536]{1,0:T(8,128)(2,1)S(1)} collective-permute-done((bf16[64,1536]{1,0:T(8,128)(2,1)S(1)}, bf16[64,1536]{1,0:T(8,128)(2,1)S(1)}, u32[]{:S(2)}, u32[]{:S(2)}) %collective-permute-start.28) | collective-permute-done | bytes 196640 | tf_op jit(solution)/shard_map/ppermute | solution.py:230
  104.3 2.1 %collective-permute-done.20.refs_7_ = bf16[64,1536]{1,0:T(8,128)(2,1)S(1)} collective-permute-done((bf16[64,1536]{1,0:T(8,128)(2,1)S(1)}, bf16[64,1536]{1,0:T(8,128)(2,1)S(1)}, u32[]{:S(2)}, u32[]{:S(2)}) %collective-permute-start.20) | collective-permute-done | bytes 196640 | tf_op jit(solution)/shard_map/ppermute | solution.py:230
  116.8 2.2 %collective-permute-done.32.refs_0_ = bf16[192,1536]{1,0:T(8,128)(2,1)} collective-permute-done((bf16[192,1536]{1,0:T(8,128)(2,1)}, bf16[192,1536]{1,0:T(8,128)(2,1)}, u32[]{:S(2)}, u32[]{:S(2)}) %collective-permute-start.32) | collective-permute-done | bytes 589856 | tf_op jit(solution)/shard_map/ppermute | solution.py:320
  120.5 2.1 %collective-permute-start.36 = (bf16[2,128,384]{2,1,0:T(8,128)(2,1)S(1)}, bf16[2,128,384]{2,1,0:T(8,128)(2,1)S(1)}, u32[]{:S(2)}, u32[]{:S(2)}) collective-permute-start(bf16[2,128,384]{2,1,0:T(8,128)(2,1)S(1)} %get-tuple-element.96), channel_id=1, source_target_pairs={{0,2},{1,3},{2,0},{3,1},{4,6},{5,7},{6,4},{7,5},{8,10},{9,11},{10,... | collective-permute-start | bytes 589832 | tf_op jit(solution)/shard_map/ppermute | solution.py:332
  126.0 5.3 %collective-permute-done.35 = bf16[2,128,384]{2,1,0:T(8,128)(2,1)S(1)} collective-permute-done((bf16[2,128,384]{2,1,0:T(8,128)(2,1)S(1)}, bf16[2,128,384]{2,1,0:T(8,128)(2,1)S(1)}, u32[]{:S(2)}, u32[]{:S(2)}) %collective-permute-start.35) | collective-permute-done | bytes 196640 | tf_op jit(solution)/shard_map/ppermute | solution.py:332
  133.6 2.9 %shard_map.67 = f32[384,1536]{1,0:T(8,128)} custom-call(bf16[384,1536]{1,0:T(8,128)(2,1)S(1)} %convolution_convert_fusion.1.here, bf16[384,1536]{1,0:T(8,128)(2,1)S(1)} %collective-permute-done.31.there, bf16[192,1536]{1,0:T(8,128)(2,1)} %collective-permute-done.32.refs_0_, bf16[192,1536]{1,0:T(8,128)(2,1)} %collective-permute-done.33.refs_1_), custom_call_target="tpu_custom_call" | custom-call | flops 1 | bytes 1 | tf_op jit(solution)/shard_map/pallas_call | solution.py:169
  (121 shorter events, 58.4 us)
Async XLA Ops:
  0.6 8.9 %collective-permute-start = (bf16[384,3072]{1,0:T(8,128)(2,1)}, bf16[384,3072]{1,0:T(8,128)(2,1)}, u32[]{:S(2)}, u32[]{:S(2)}) collective-permute-start(bf16[384,3072]{1,0:T(8,128)(2,1)} %param.4), channel_id=1, source_target_pairs={{0,8},{8,0},{1,9},{9,1},{2,10},{10,2},{3,11},{11,3},{4,12},{12,4},... | collective-permute-start | bytes 7077896 | tf_op jit(solution)/shard_map/ppermute | solution.py:227
  2.6 17.9 %all-to-all-start = ((bf16[8,128,384]{2,1,0:T(8,128)(2,1)}), bf16[8,128,384]{2,1,0:T(8,128)(2,1)S(1)}, u32[]{:S(2)}, u32[]{:S(2)}) async-start(bf16[8,128,384]{2,1,0:T(8,128)(2,1)} %shard_map.58), calls=%async_computation | async-start | bytes 1572864 | tf_op jit(solution)/shard_map/all_to_all | solution.py:242
  23.0 9.6 %collective-permute-start.7 = (bf16[64,1536]{1,0:T(8,128)(2,1)S(1)}, bf16[64,1536]{1,0:T(8,128)(2,1)S(1)}, u32[]{:S(2)}, u32[]{:S(2)}) collective-permute-start(bf16[64,1536]{1,0:T(8,128)(2,1)S(1)} %convolution_convert_fusion.4), channel_id=1, source_target_pairs={{0,16},{16,32},{32,48},{48,64},{64,80},{80,96},{96,112},{112,0},{8... | collective-permute-start | bytes 589832 | tf_op jit(solution)/shard_map/ppermute | solution.py:230
  32.6 9.1 %collective-permute-start.8 = (bf16[128,1536]{1,0:T(8,128)(2,1)S(1)}, bf16[128,1536]{1,0:T(8,128)(2,1)S(1)}, u32[]{:S(2)}, u32[]{:S(2)}) collective-permute-start(bf16[128,1536]{1,0:T(8,128)(2,1)S(1)} %fusion), channel_id=1, source_target_pairs={{0,16},{16,32},{32,48},{48,64},{64,80},{80,96},{96,112},{112,0},{8... | collective-permute-start | bytes 1179656 | tf_op jit(solution)/shard_map/ppermute | solution.py:230
  35.0 10.9 %collective-permute-start.4 = (bf16[128,1536]{1,0:T(8,128)(2,1)S(1)}, bf16[128,1536]{1,0:T(8,128)(2,1)S(1)}, u32[]{:S(2)}, u32[]{:S(2)}) collective-permute-start(bf16[128,1536]{1,0:T(8,128)(2,1)S(1)} %fusion.3), channel_id=1, source_target_pairs={{0,16},{16,32},{32,48},{48,64},{64,80},{80,96},{96,112},{112,0},{8... | collective-permute-start | bytes 1179656 | tf_op jit(solution)/shard_map/ppermute | solution.py:230
  41.8 9.1 %collective-permute-start.9 = (bf16[128,1536]{1,0:T(8,128)(2,1)S(1)}, bf16[128,1536]{1,0:T(8,128)(2,1)S(1)}, u32[]{:S(2)}, u32[]{:S(2)}) collective-permute-start(bf16[128,1536]{1,0:T(8,128)(2,1)S(1)} %fusion.1), channel_id=1, source_target_pairs={{0,16},{16,32},{32,48},{48,64},{64,80},{80,96},{96,112},{112,0},{8... | collective-permute-start | bytes 1179656 | tf_op jit(solution)/shard_map/ppermute | solution.py:230
  45.9 9.1 %collective-permute-start.5 = (bf16[128,1536]{1,0:T(8,128)(2,1)S(1)}, bf16[128,1536]{1,0:T(8,128)(2,1)S(1)}, u32[]{:S(2)}, u32[]{:S(2)}) collective-permute-start(bf16[128,1536]{1,0:T(8,128)(2,1)S(1)} %fusion.4), channel_id=1, source_target_pairs={{0,16},{16,32},{32,48},{48,64},{64,80},{80,96},{96,112},{112,0},{8... | collective-permute-start | bytes 1179656 | tf_op jit(solution)/shard_map/ppermute | solution.py:230
  50.9 9.1 %collective-permute-start.10 = (bf16[128,1536]{1,0:T(8,128)(2,1)S(1)}, bf16[128,1536]{1,0:T(8,128)(2,1)S(1)}, u32[]{:S(2)}, u32[]{:S(2)}) collective-permute-start(bf16[128,1536]{1,0:T(8,128)(2,1)S(1)} %fusion.2), channel_id=1, source_target_pairs={{0,16},{16,32},{32,48},{48,64},{64,80},{80,96},{96,112},{112,0},{8... | collective-permute-start | bytes 1179656 | tf_op jit(solution)/shard_map/ppermute | solution.py:230
  55.1 9.1 %collective-permute-start.6 = (bf16[128,1536]{1,0:T(8,128)(2,1)S(1)}, bf16[128,1536]{1,0:T(8,128)(2,1)S(1)}, u32[]{:S(2)}, u32[]{:S(2)}) collective-permute-start(bf16[128,1536]{1,0:T(8,128)(2,1)S(1)} %fusion.5), channel_id=1, source_target_pairs={{0,16},{16,32},{32,48},{48,64},{64,80},{80,96},{96,112},{112,0},{8... | collective-permute-start | bytes 1179656 | tf_op jit(solution)/shard_map/ppermute | solution.py:230
  67.8 8.3 %collective-permute-start.24 = (bf16[64,1536]{1,0:T(8,128)(2,1)S(1)}, bf16[64,1536]{1,0:T(8,128)(2,1)S(1)}, u32[]{:S(2)}, u32[]{:S(2)}) collective-permute-start(bf16[64,1536]{1,0:T(8,128)(2,1)S(1)} %collective-permute-done.23), channel_id=1, source_target_pairs={{0,16},{16,32},{32,48},{48,64},{64,80},{80,96},{96,112},{112,0},{8... | collective-permute-start | bytes 589832 | tf_op jit(solution)/shard_map/ppermute | solution.py:230
  72.4 10.2 %collective-permute-start.16 = (bf16[64,1536]{1,0:T(8,128)(2,1)S(1)}, bf16[64,1536]{1,0:T(8,128)(2,1)S(1)}, u32[]{:S(2)}, u32[]{:S(2)}) collective-permute-start(bf16[64,1536]{1,0:T(8,128)(2,1)S(1)} %collective-permute-done.15), channel_id=1, source_target_pairs={{0,16},{16,32},{32,48},{48,64},{64,80},{80,96},{96,112},{112,0},{8... | collective-permute-start | bytes 589832 | tf_op jit(solution)/shard_map/ppermute | solution.py:230
  74.0 8.6 %collective-permute-start.14 = (bf16[64,1536]{1,0:T(8,128)(2,1)S(1)}, bf16[64,1536]{1,0:T(8,128)(2,1)S(1)}, u32[]{:S(2)}, u32[]{:S(2)}) collective-permute-start(bf16[64,1536]{1,0:T(8,128)(2,1)S(1)} %collective-permute-done.13.refs_1_), channel_id=1, source_target_pairs={{0,16},{16,32},{32,48},{48,64},{64,80},{80,96},{96,112},{112,0},{8... | collective-permute-start | bytes 589832 | tf_op jit(solution)/shard_map/ppermute | solution.py:230
  76.1 10.7 %collective-permute-start.26 = (bf16[64,1536]{1,0:T(8,128)(2,1)S(1)}, bf16[64,1536]{1,0:T(8,128)(2,1)S(1)}, u32[]{:S(2)}, u32[]{:S(2)}) collective-permute-start(bf16[64,1536]{1,0:T(8,128)(2,1)S(1)} %collective-permute-done.24.refs_3_), channel_id=1, source_target_pairs={{0,16},{16,32},{32,48},{48,64},{64,80},{80,96},{96,112},{112,0},{8... | collective-permute-start | bytes 589832 | tf_op jit(solution)/shard_map/ppermute | solution.py:230
  78.3 8.4 %collective-permute-start.25 = (bf16[64,1536]{1,0:T(8,128)(2,1)S(1)}, bf16[64,1536]{1,0:T(8,128)(2,1)S(1)}, u32[]{:S(2)}, u32[]{:S(2)}) collective-permute-start(bf16[64,1536]{1,0:T(8,128)(2,1)S(1)} %collective-permute-done.22.refs_2_), channel_id=1, source_target_pairs={{0,16},{16,32},{32,48},{48,64},{64,80},{80,96},{96,112},{112,0},{8... | collective-permute-start | bytes 589832 | tf_op jit(solution)/shard_map/ppermute | solution.py:230
  79.1 17.1 %collective-permute-start.29 = (bf16[512,384]{1,0:T(8,128)(2,1)S(1)}, bf16[512,384]{1,0:T(8,128)(2,1)S(1)}, u32[]{:S(2)}, u32[]{:S(2)}) collective-permute-start(bf16[512,384]{1,0:T(8,128)(2,1)S(1)} %get-tuple-element.73), channel_id=1, source_target_pairs={{0,8},{8,0},{1,9},{9,1},{2,10},{10,2},{3,11},{11,3},{4,12},{12,4},... | collective-permute-start | bytes 1179656 | tf_op jit(solution)/shard_map/ppermute | solution.py:227
  82.5 9.0 %collective-permute-start.18 = (bf16[64,1536]{1,0:T(8,128)(2,1)S(1)}, bf16[64,1536]{1,0:T(8,128)(2,1)S(1)}, u32[]{:S(2)}, u32[]{:S(2)}) collective-permute-start(bf16[64,1536]{1,0:T(8,128)(2,1)S(1)} %collective-permute-done.16.refs_3_), channel_id=1, source_target_pairs={{0,16},{16,32},{32,48},{48,64},{64,80},{80,96},{96,112},{112,0},{8... | collective-permute-start | bytes 589832 | tf_op jit(solution)/shard_map/ppermute | solution.py:230
  86.8 9.0 %collective-permute-start.28 = (bf16[64,1536]{1,0:T(8,128)(2,1)S(1)}, bf16[64,1536]{1,0:T(8,128)(2,1)S(1)}, u32[]{:S(2)}, u32[]{:S(2)}) collective-permute-start(bf16[64,1536]{1,0:T(8,128)(2,1)S(1)} %collective-permute-done.26.refs_5_), channel_id=1, source_target_pairs={{0,16},{16,32},{32,48},{48,64},{64,80},{80,96},{96,112},{112,0},{8... | collective-permute-start | bytes 589832 | tf_op jit(solution)/shard_map/ppermute | solution.py:230
  97.4 9.0 %collective-permute-start.20 = (bf16[64,1536]{1,0:T(8,128)(2,1)S(1)}, bf16[64,1536]{1,0:T(8,128)(2,1)S(1)}, u32[]{:S(2)}, u32[]{:S(2)}) collective-permute-start(bf16[64,1536]{1,0:T(8,128)(2,1)S(1)} %collective-permute-done.18.refs_5_), channel_id=1, source_target_pairs={{0,16},{16,32},{32,48},{48,64},{64,80},{80,96},{96,112},{112,0},{8... | collective-permute-start | bytes 589832 | tf_op jit(solution)/shard_map/ppermute | solution.py:230
  101.7 17.2 %collective-permute-start.32 = (bf16[192,1536]{1,0:T(8,128)(2,1)}, bf16[192,1536]{1,0:T(8,128)(2,1)}, u32[]{:S(2)}, u32[]{:S(2)}) collective-permute-start(bf16[192,1536]{1,0:T(8,128)(2,1)} %get-tuple-element.74), channel_id=1, source_target_pairs={{0,128},{128,0},{1,129},{129,1},{2,130},{130,2},{3,131},{131,3},{4... | collective-permute-start | bytes 1769480 | tf_op jit(solution)/shard_map/ppermute | solution.py:320
  113.1 18.8 %collective-permute-start.31 = (bf16[384,1536]{1,0:T(8,128)(2,1)}, bf16[384,1536]{1,0:T(8,128)(2,1)S(1)}, u32[]{:S(2)}, u32[]{:S(2)}) collective-permute-start(bf16[384,1536]{1,0:T(8,128)(2,1)} %convolution_convert_fusion), channel_id=1, source_target_pairs={{0,8},{8,0},{1,9},{9,1},{2,10},{10,2},{3,11},{11,3},{4,12},{12,4},... | collective-permute-start | bytes 3538952 | tf_op jit(solution)/shard_map/ppermute | solution.py:227
  114.5 17.5 %collective-permute-start.33 = (bf16[192,1536]{1,0:T(8,128)(2,1)}, bf16[192,1536]{1,0:T(8,128)(2,1)}, u32[]{:S(2)}, u32[]{:S(2)}) collective-permute-start(bf16[192,1536]{1,0:T(8,128)(2,1)} %copy-done.2), channel_id=1, source_target_pairs={{0,128},{128,0},{1,129},{129,1},{2,130},{130,2},{3,131},{131,3},{4... | collective-permute-start | bytes 1769480 | tf_op jit(solution)/shard_map/ppermute | solution.py:320
  119.6 11.6 %collective-permute-start.35 = (bf16[2,128,384]{2,1,0:T(8,128)(2,1)S(1)}, bf16[2,128,384]{2,1,0:T(8,128)(2,1)S(1)}, u32[]{:S(2)}, u32[]{:S(2)}) collective-permute-start(bf16[2,128,384]{2,1,0:T(8,128)(2,1)S(1)} %get-tuple-element.95), channel_id=1, source_target_pairs={{0,1},{1,2},{2,3},{3,0},{4,5},{5,6},{6,7},{7,4},{8,9},{9,10},{10,1... | collective-permute-start | bytes 589832 | tf_op jit(solution)/shard_map/ppermute | solution.py:332
  120.5 10.7 %collective-permute-start.36 = (bf16[2,128,384]{2,1,0:T(8,128)(2,1)S(1)}, bf16[2,128,384]{2,1,0:T(8,128)(2,1)S(1)}, u32[]{:S(2)}, u32[]{:S(2)}) collective-permute-start(bf16[2,128,384]{2,1,0:T(8,128)(2,1)S(1)} %get-tuple-element.96), channel_id=1, source_target_pairs={{0,2},{1,3},{2,0},{3,1},{4,6},{5,7},{6,4},{7,5},{8,10},{9,11},{10,... | collective-permute-start | bytes 589832 | tf_op jit(solution)/shard_map/ppermute | solution.py:332
  122.7 9.2 %collective-permute-start.37 = (bf16[2,128,384]{2,1,0:T(8,128)(2,1)S(1)}, bf16[2,128,384]{2,1,0:T(8,128)(2,1)S(1)}, u32[]{:S(2)}, u32[]{:S(2)}) collective-permute-start(bf16[2,128,384]{2,1,0:T(8,128)(2,1)S(1)} %get-tuple-element.97), channel_id=1, source_target_pairs={{0,3},{1,0},{2,1},{3,2},{4,7},{5,4},{6,5},{7,6},{8,11},{9,8},{10,9... | collective-permute-start | bytes 589832 | tf_op jit(solution)/shard_map/ppermute | solution.py:332
  (27 other events, 154.7 us)

commit v3 on v2

--- a/solution.py
+++ b/solution.py
@@ -111,15 +111,20 @@
 
 
 def copies(value, count):
-    def body(value, out):
-        for i in range(count):
-            out[i] = value[...]
-
-    return pl.pallas_call(
-        body,
-        in_specs=[VMEM],
-        out_specs=VMEM,
+    def body(value, out, sems):
+        moves = [pltpu.make_async_copy(value, out.at[i], sems.at[i]) for i in range(count)]
+        for move in moves:
+            move.start()
+        for move in moves:
+            move.wait()
+
+    anywhere = pl.BlockSpec(memory_space=pl.ANY)
+    return pl.pallas_call(
+        body,
+        in_specs=[anywhere],
+        out_specs=anywhere,
         out_shape=jax.ShapeDtypeStruct((count,) + value.shape, value.dtype),
+        scratch_shapes=[pltpu.SemaphoreType.DMA((count,))],
         **PARAMS,
     )(value)
 

time: 138 us -> 138 us (level)
  no operation moved by 1% of the time
where the time goes in v3:
time: 138 us; the launch traced here: 137 us
  waiting for transfers between devices  71.6 us (52%)
  starting transfers between devices  32 us (23%)
  matrix products  11.5 us (8%)
  Pallas kernels  10.8 us (8%)
  local copies, waits for them, and re-layouts  7.61 us (6%)
  other arithmetic  2.83 us (2%)
    ppermute x22, waiting for transfers between devices, along(): return lax.ppermute(value, ('z', 'core'), ring)  51.3 us
    ppermute x22, starting transfers between devices, along(): return lax.ppermute(value, ('z', 'core'), ring)  15.7 us
    dot_general x10, matrix products, dot(): return lax.dot_general(a, b, (over, ((), ())), preferred_element_type=F32)  11.5 us
    all_to_all x1, waiting for transfers between devices, shards(): lax.all_to_all(copies(tokens, ncol), ('xl', 'y'), 0, 0)  7.05 us
    ppermute x3, waiting for transfers between devices, shards(): lax.ppermute(for_y[hop], 'y', [(i, (i + hop) % ny) for i in range(ny)])  5.85 us
    all_to_all x1, starting transfers between devices, shards(): lax.all_to_all(copies(tokens, ncol), ('xl', 'y'), 0, 0)  5.25 us
    ppermute x11, waiting for transfers between devices, swap(): return lax.ppermute(value, 'core', SWAP)  5.02 us
    ppermute x3, starting transfers between devices, shards(): lax.ppermute(for_y[hop], 'y', [(i, (i + hop) % ny) for i in range(ny)])  4.56 us
  transfers between devices with their start and end apart: 40, of which 30 were waited for; matrix products, arithmetic and copies ran while one was open for 13% of the time, Pallas kernels for 7%

profile of v3, /device:TPU:4, one launch (start us, length us, event | category | flops | bytes accessed | tf_op | source)
XLA Modules:
  0.0 137.4 jit_solution(12937416789137041403)
XLA Ops:
  2.6 5.2 %all-to-all-start = ((bf16[8,128,384]{2,1,0:T(8,128)(2,1)}), bf16[8,128,384]{2,1,0:T(8,128)(2,1)S(1)}, u32[]{:S(2)}, u32[]{:S(2)}) async-start(bf16[8,128,384]{2,1,0:T(8,128)(2,1)} %shard_map.58), calls=%async_computation | async-start | bytes 1572864 | tf_op jit(solution)/shard_map/all_to_all | solution.py:247
  9.6 1.9 %constant_dynamic-slice_fusion = (bf16[384,1536]{1,0:T(8,128)(2,1)S(1)}, bf16[384,1536]{1,0:T(8,128)(2,1)S(1)}) fusion(bf16[384,3072]{1,0:T(8,128)(2,1)} %collective-permute-done, s32[]{:T(128)S(6)} %select_n.123, s32[]{:T(128)S(6)} %select_n.122), kind=kLoop, calls=%fused_computation.29 | loop fusion | bytes 4718600 | tf_op jit(solution)/shard_map/dynamic_slice | solution.py:22
  13.4 7.1 %all-to-all-done = bf16[8,128,384]{2,1,0:T(8,128)(2,1)S(1)} async-done(((bf16[8,128,384]{2,1,0:T(8,128)(2,1)}), bf16[8,128,384]{2,1,0:T(8,128)(2,1)S(1)}, u32[]{:S(2)}, u32[]{:S(2)}) %all-to-all-start) | async-done | bytes 786464 | tf_op jit(solution)/shard_map/all_to_all | solution.py:247
  23.0 2.0 %collective-permute-start.7 = (bf16[64,1536]{1,0:T(8,128)(2,1)S(1)}, bf16[64,1536]{1,0:T(8,128)(2,1)S(1)}, u32[]{:S(2)}, u32[]{:S(2)}) collective-permute-start(bf16[64,1536]{1,0:T(8,128)(2,1)S(1)} %convolution_convert_fusion.4), channel_id=1, source_target_pairs={{0,16},{16,32},{32,48},{48,64},{64,80},{80,96},{96,112},{112,0},{8... | collective-permute-start | bytes 589832 | tf_op jit(solution)/shard_map/ppermute | solution.py:235
  27.2 2.0 %collective-permute-start.3 = (bf16[64,1536]{1,0:T(8,128)(2,1)S(1)}, bf16[64,1536]{1,0:T(8,128)(2,1)S(1)}, u32[]{:S(2)}, u32[]{:S(2)}) collective-permute-start(bf16[64,1536]{1,0:T(8,128)(2,1)S(1)} %convolution_convert_fusion.5), channel_id=1, source_target_pairs={{0,16},{16,32},{32,48},{48,64},{64,80},{80,96},{96,112},{112,0},{8... | collective-permute-start | bytes 589832 | tf_op jit(solution)/shard_map/ppermute | solution.py:235
  29.2 3.3 %collective-permute-done.7 = bf16[64,1536]{1,0:T(8,128)(2,1)S(1)} collective-permute-done((bf16[64,1536]{1,0:T(8,128)(2,1)S(1)}, bf16[64,1536]{1,0:T(8,128)(2,1)S(1)}, u32[]{:S(2)}, u32[]{:S(2)}) %collective-permute-start.7) | collective-permute-done | bytes 196640 | tf_op jit(solution)/shard_map/ppermute | solution.py:235
  35.8 5.9 %collective-permute-done.8 = bf16[128,1536]{1,0:T(8,128)(2,1)S(1)} collective-permute-done((bf16[128,1536]{1,0:T(8,128)(2,1)S(1)}, bf16[128,1536]{1,0:T(8,128)(2,1)S(1)}, u32[]{:S(2)}, u32[]{:S(2)}) %collective-permute-start.8) | collective-permute-done | bytes 393248 | tf_op jit(solution)/shard_map/ppermute | solution.py:235
  41.9 4.0 %collective-permute-done.4 = bf16[128,1536]{1,0:T(8,128)(2,1)S(1)} collective-permute-done((bf16[128,1536]{1,0:T(8,128)(2,1)S(1)}, bf16[128,1536]{1,0:T(8,128)(2,1)S(1)}, u32[]{:S(2)}, u32[]{:S(2)}) %collective-permute-start.4) | collective-permute-done | bytes 393248 | tf_op jit(solution)/shard_map/ppermute | solution.py:235
  46.1 4.8 %collective-permute-done.9 = bf16[128,1536]{1,0:T(8,128)(2,1)S(1)} collective-permute-done((bf16[128,1536]{1,0:T(8,128)(2,1)S(1)}, bf16[128,1536]{1,0:T(8,128)(2,1)S(1)}, u32[]{:S(2)}, u32[]{:S(2)}) %collective-permute-start.9) | collective-permute-done | bytes 393248 | tf_op jit(solution)/shard_map/ppermute | solution.py:235
  51.0 4.0 %collective-permute-done.5 = bf16[128,1536]{1,0:T(8,128)(2,1)S(1)} collective-permute-done((bf16[128,1536]{1,0:T(8,128)(2,1)S(1)}, bf16[128,1536]{1,0:T(8,128)(2,1)S(1)}, u32[]{:S(2)}, u32[]{:S(2)}) %collective-permute-start.5) | collective-permute-done | bytes 393248 | tf_op jit(solution)/shard_map/ppermute | solution.py:235
  55.2 4.8 %collective-permute-done.10.mine = bf16[128,1536]{1,0:T(8,128)(2,1)S(1)} collective-permute-done((bf16[128,1536]{1,0:T(8,128)(2,1)S(1)}, bf16[128,1536]{1,0:T(8,128)(2,1)S(1)}, u32[]{:S(2)}, u32[]{:S(2)}) %collective-permute-start.10) | collective-permute-done | bytes 393248 | tf_op jit(solution)/shard_map/ppermute | solution.py:235
  68.7 2.8 %collective-permute-done.21.refs_1_ = bf16[64,1536]{1,0:T(8,128)(2,1)S(1)} collective-permute-done((bf16[64,1536]{1,0:T(8,128)(2,1)S(1)}, bf16[64,1536]{1,0:T(8,128)(2,1)S(1)}, u32[]{:S(2)}, u32[]{:S(2)}) %collective-permute-start.21) | collective-permute-done | bytes 196640 | tf_op jit(solution)/shard_map/ppermute | solution.py:235
  74.1 2.0 %collective-permute-done.24.refs_3_ = bf16[64,1536]{1,0:T(8,128)(2,1)S(1)} collective-permute-done((bf16[64,1536]{1,0:T(8,128)(2,1)S(1)}, bf16[64,1536]{1,0:T(8,128)(2,1)S(1)}, u32[]{:S(2)}, u32[]{:S(2)}) %collective-permute-start.24) | collective-permute-done | bytes 196640 | tf_op jit(solution)/shard_map/ppermute | solution.py:235
  79.9 2.7 %collective-permute-done.14.refs_2_ = bf16[64,1536]{1,0:T(8,128)(2,1)S(1)} collective-permute-done((bf16[64,1536]{1,0:T(8,128)(2,1)S(1)}, bf16[64,1536]{1,0:T(8,128)(2,1)S(1)}, u32[]{:S(2)}, u32[]{:S(2)}) %collective-permute-start.14) | collective-permute-done | bytes 196640 | tf_op jit(solution)/shard_map/ppermute | solution.py:235
  84.4 2.4 %collective-permute-done.25.refs_4_ = bf16[64,1536]{1,0:T(8,128)(2,1)S(1)} collective-permute-done((bf16[64,1536]{1,0:T(8,128)(2,1)S(1)}, bf16[64,1536]{1,0:T(8,128)(2,1)S(1)}, u32[]{:S(2)}, u32[]{:S(2)}) %collective-permute-start.25) | collective-permute-done | bytes 196640 | tf_op jit(solution)/shard_map/ppermute | solution.py:235
  86.8 2.1 %collective-permute-start.28 = (bf16[64,1536]{1,0:T(8,128)(2,1)S(1)}, bf16[64,1536]{1,0:T(8,128)(2,1)S(1)}, u32[]{:S(2)}, u32[]{:S(2)}) collective-permute-start(bf16[64,1536]{1,0:T(8,128)(2,1)S(1)} %collective-permute-done.26.refs_5_), channel_id=1, source_target_pairs={{0,16},{16,32},{32,48},{48,64},{64,80},{80,96},{96,112},{112,0},{8... | collective-permute-start | bytes 589832 | tf_op jit(solution)/shard_map/ppermute | solution.py:235
  89.4 2.1 %collective-permute-done.18.refs_5_ = bf16[64,1536]{1,0:T(8,128)(2,1)S(1)} collective-permute-done((bf16[64,1536]{1,0:T(8,128)(2,1)S(1)}, bf16[64,1536]{1,0:T(8,128)(2,1)S(1)}, u32[]{:S(2)}, u32[]{:S(2)}) %collective-permute-start.18) | collective-permute-done | bytes 196640 | tf_op jit(solution)/shard_map/ppermute | solution.py:235
  91.5 2.1 %collective-permute-done.27.refs_6_ = bf16[64,1536]{1,0:T(8,128)(2,1)S(1)} collective-permute-done((bf16[64,1536]{1,0:T(8,128)(2,1)S(1)}, bf16[64,1536]{1,0:T(8,128)(2,1)S(1)}, u32[]{:S(2)}, u32[]{:S(2)}) %collective-permute-start.27) | collective-permute-done | bytes 196640 | tf_op jit(solution)/shard_map/ppermute | solution.py:235
  93.7 2.1 %collective-permute-done.28.refs_7_ = bf16[64,1536]{1,0:T(8,128)(2,1)S(1)} collective-permute-done((bf16[64,1536]{1,0:T(8,128)(2,1)S(1)}, bf16[64,1536]{1,0:T(8,128)(2,1)S(1)}, u32[]{:S(2)}, u32[]{:S(2)}) %collective-permute-start.28) | collective-permute-done | bytes 196640 | tf_op jit(solution)/shard_map/ppermute | solution.py:235
  104.3 2.1 %collective-permute-done.20.refs_7_ = bf16[64,1536]{1,0:T(8,128)(2,1)S(1)} collective-permute-done((bf16[64,1536]{1,0:T(8,128)(2,1)S(1)}, bf16[64,1536]{1,0:T(8,128)(2,1)S(1)}, u32[]{:S(2)}, u32[]{:S(2)}) %collective-permute-start.20) | collective-permute-done | bytes 196640 | tf_op jit(solution)/shard_map/ppermute | solution.py:235
  116.8 2.2 %collective-permute-done.32.refs_0_ = bf16[192,1536]{1,0:T(8,128)(2,1)} collective-permute-done((bf16[192,1536]{1,0:T(8,128)(2,1)}, bf16[192,1536]{1,0:T(8,128)(2,1)}, u32[]{:S(2)}, u32[]{:S(2)}) %collective-permute-start.32) | collective-permute-done | bytes 589856 | tf_op jit(solution)/shard_map/ppermute | solution.py:325
  120.6 2.1 %collective-permute-start.36 = (bf16[2,128,384]{2,1,0:T(8,128)(2,1)S(1)}, bf16[2,128,384]{2,1,0:T(8,128)(2,1)S(1)}, u32[]{:S(2)}, u32[]{:S(2)}) collective-permute-start(bf16[2,128,384]{2,1,0:T(8,128)(2,1)S(1)} %get-tuple-element.96), channel_id=1, source_target_pairs={{0,2},{1,3},{2,0},{3,1},{4,6},{5,7},{6,4},{7,5},{8,10},{9,11},{10,... | collective-permute-start | bytes 589832 | tf_op jit(solution)/shard_map/ppermute | solution.py:337
  126.0 5.3 %collective-permute-done.35 = bf16[2,128,384]{2,1,0:T(8,128)(2,1)S(1)} collective-permute-done((bf16[2,128,384]{2,1,0:T(8,128)(2,1)S(1)}, bf16[2,128,384]{2,1,0:T(8,128)(2,1)S(1)}, u32[]{:S(2)}, u32[]{:S(2)}) %collective-permute-start.35) | collective-permute-done | bytes 196640 | tf_op jit(solution)/shard_map/ppermute | solution.py:337
  133.6 2.9 %shard_map.67 = f32[384,1536]{1,0:T(8,128)} custom-call(bf16[384,1536]{1,0:T(8,128)(2,1)S(1)} %convolution_convert_fusion.1.here, bf16[384,1536]{1,0:T(8,128)(2,1)S(1)} %collective-permute-done.31.there, bf16[192,1536]{1,0:T(8,128)(2,1)} %collective-permute-done.32.refs_0_, bf16[192,1536]{1,0:T(8,128)(2,1)} %collective-permute-done.33.refs_1_), custom_call_target="tpu_custom_call" | custom-call | flops 1 | bytes 1 | tf_op jit(solution)/shard_map/pallas_call | solution.py:174
  (121 shorter events, 58.4 us)
Async XLA Ops:
  0.6 8.9 %collective-permute-start = (bf16[384,3072]{1,0:T(8,128)(2,1)}, bf16[384,3072]{1,0:T(8,128)(2,1)}, u32[]{:S(2)}, u32[]{:S(2)}) collective-permute-start(bf16[384,3072]{1,0:T(8,128)(2,1)} %param.4), channel_id=1, source_target_pairs={{0,8},{8,0},{1,9},{9,1},{2,10},{10,2},{3,11},{11,3},{4,12},{12,4},... | collective-permute-start | bytes 7077896 | tf_op jit(solution)/shard_map/ppermute | solution.py:232
  2.6 17.9 %all-to-all-start = ((bf16[8,128,384]{2,1,0:T(8,128)(2,1)}), bf16[8,128,384]{2,1,0:T(8,128)(2,1)S(1)}, u32[]{:S(2)}, u32[]{:S(2)}) async-start(bf16[8,128,384]{2,1,0:T(8,128)(2,1)} %shard_map.58), calls=%async_computation | async-start | bytes 1572864 | tf_op jit(solution)/shard_map/all_to_all | solution.py:247
  23.0 9.6 %collective-permute-start.7 = (bf16[64,1536]{1,0:T(8,128)(2,1)S(1)}, bf16[64,1536]{1,0:T(8,128)(2,1)S(1)}, u32[]{:S(2)}, u32[]{:S(2)}) collective-permute-start(bf16[64,1536]{1,0:T(8,128)(2,1)S(1)} %convolution_convert_fusion.4), channel_id=1, source_target_pairs={{0,16},{16,32},{32,48},{48,64},{64,80},{80,96},{96,112},{112,0},{8... | collective-permute-start | bytes 589832 | tf_op jit(solution)/shard_map/ppermute | solution.py:235
  32.6 9.1 %collective-permute-start.8 = (bf16[128,1536]{1,0:T(8,128)(2,1)S(1)}, bf16[128,1536]{1,0:T(8,128)(2,1)S(1)}, u32[]{:S(2)}, u32[]{:S(2)}) collective-permute-start(bf16[128,1536]{1,0:T(8,128)(2,1)S(1)} %fusion), channel_id=1, source_target_pairs={{0,16},{16,32},{32,48},{48,64},{64,80},{80,96},{96,112},{112,0},{8... | collective-permute-start | bytes 1179656 | tf_op jit(solution)/shard_map/ppermute | solution.py:235
  35.0 10.9 %collective-permute-start.4 = (bf16[128,1536]{1,0:T(8,128)(2,1)S(1)}, bf16[128,1536]{1,0:T(8,128)(2,1)S(1)}, u32[]{:S(2)}, u32[]{:S(2)}) collective-permute-start(bf16[128,1536]{1,0:T(8,128)(2,1)S(1)} %fusion.3), channel_id=1, source_target_pairs={{0,16},{16,32},{32,48},{48,64},{64,80},{80,96},{96,112},{112,0},{8... | collective-permute-start | bytes 1179656 | tf_op jit(solution)/shard_map/ppermute | solution.py:235
  41.8 9.1 %collective-permute-start.9 = (bf16[128,1536]{1,0:T(8,128)(2,1)S(1)}, bf16[128,1536]{1,0:T(8,128)(2,1)S(1)}, u32[]{:S(2)}, u32[]{:S(2)}) collective-permute-start(bf16[128,1536]{1,0:T(8,128)(2,1)S(1)} %fusion.1), channel_id=1, source_target_pairs={{0,16},{16,32},{32,48},{48,64},{64,80},{80,96},{96,112},{112,0},{8... | collective-permute-start | bytes 1179656 | tf_op jit(solution)/shard_map/ppermute | solution.py:235
  46.0 9.1 %collective-permute-start.5 = (bf16[128,1536]{1,0:T(8,128)(2,1)S(1)}, bf16[128,1536]{1,0:T(8,128)(2,1)S(1)}, u32[]{:S(2)}, u32[]{:S(2)}) collective-permute-start(bf16[128,1536]{1,0:T(8,128)(2,1)S(1)} %fusion.4), channel_id=1, source_target_pairs={{0,16},{16,32},{32,48},{48,64},{64,80},{80,96},{96,112},{112,0},{8... | collective-permute-start | bytes 1179656 | tf_op jit(solution)/shard_map/ppermute | solution.py:235
  50.9 9.1 %collective-permute-start.10 = (bf16[128,1536]{1,0:T(8,128)(2,1)S(1)}, bf16[128,1536]{1,0:T(8,128)(2,1)S(1)}, u32[]{:S(2)}, u32[]{:S(2)}) collective-permute-start(bf16[128,1536]{1,0:T(8,128)(2,1)S(1)} %fusion.2), channel_id=1, source_target_pairs={{0,16},{16,32},{32,48},{48,64},{64,80},{80,96},{96,112},{112,0},{8... | collective-permute-start | bytes 1179656 | tf_op jit(solution)/shard_map/ppermute | solution.py:235
  55.1 9.1 %collective-permute-start.6 = (bf16[128,1536]{1,0:T(8,128)(2,1)S(1)}, bf16[128,1536]{1,0:T(8,128)(2,1)S(1)}, u32[]{:S(2)}, u32[]{:S(2)}) collective-permute-start(bf16[128,1536]{1,0:T(8,128)(2,1)S(1)} %fusion.5), channel_id=1, source_target_pairs={{0,16},{16,32},{32,48},{48,64},{64,80},{80,96},{96,112},{112,0},{8... | collective-permute-start | bytes 1179656 | tf_op jit(solution)/shard_map/ppermute | solution.py:235
  67.8 8.3 %collective-permute-start.24 = (bf16[64,1536]{1,0:T(8,128)(2,1)S(1)}, bf16[64,1536]{1,0:T(8,128)(2,1)S(1)}, u32[]{:S(2)}, u32[]{:S(2)}) collective-permute-start(bf16[64,1536]{1,0:T(8,128)(2,1)S(1)} %collective-permute-done.23), channel_id=1, source_target_pairs={{0,16},{16,32},{32,48},{48,64},{64,80},{80,96},{96,112},{112,0},{8... | collective-permute-start | bytes 589832 | tf_op jit(solution)/shard_map/ppermute | solution.py:235
  72.4 10.2 %collective-permute-start.16 = (bf16[64,1536]{1,0:T(8,128)(2,1)S(1)}, bf16[64,1536]{1,0:T(8,128)(2,1)S(1)}, u32[]{:S(2)}, u32[]{:S(2)}) collective-permute-start(bf16[64,1536]{1,0:T(8,128)(2,1)S(1)} %collective-permute-done.15), channel_id=1, source_target_pairs={{0,16},{16,32},{32,48},{48,64},{64,80},{80,96},{96,112},{112,0},{8... | collective-permute-start | bytes 589832 | tf_op jit(solution)/shard_map/ppermute | solution.py:235
  74.0 8.6 %collective-permute-start.14 = (bf16[64,1536]{1,0:T(8,128)(2,1)S(1)}, bf16[64,1536]{1,0:T(8,128)(2,1)S(1)}, u32[]{:S(2)}, u32[]{:S(2)}) collective-permute-start(bf16[64,1536]{1,0:T(8,128)(2,1)S(1)} %collective-permute-done.13.refs_1_), channel_id=1, source_target_pairs={{0,16},{16,32},{32,48},{48,64},{64,80},{80,96},{96,112},{112,0},{8... | collective-permute-start | bytes 589832 | tf_op jit(solution)/shard_map/ppermute | solution.py:235
  76.1 10.7 %collective-permute-start.26 = (bf16[64,1536]{1,0:T(8,128)(2,1)S(1)}, bf16[64,1536]{1,0:T(8,128)(2,1)S(1)}, u32[]{:S(2)}, u32[]{:S(2)}) collective-permute-start(bf16[64,1536]{1,0:T(8,128)(2,1)S(1)} %collective-permute-done.24.refs_3_), channel_id=1, source_target_pairs={{0,16},{16,32},{32,48},{48,64},{64,80},{80,96},{96,112},{112,0},{8... | collective-permute-start | bytes 589832 | tf_op jit(solution)/shard_map/ppermute | solution.py:235
  78.3 8.4 %collective-permute-start.25 = (bf16[64,1536]{1,0:T(8,128)(2,1)S(1)}, bf16[64,1536]{1,0:T(8,128)(2,1)S(1)}, u32[]{:S(2)}, u32[]{:S(2)}) collective-permute-start(bf16[64,1536]{1,0:T(8,128)(2,1)S(1)} %collective-permute-done.22.refs_2_), channel_id=1, source_target_pairs={{0,16},{16,32},{32,48},{48,64},{64,80},{80,96},{96,112},{112,0},{8... | collective-permute-start | bytes 589832 | tf_op jit(solution)/shard_map/ppermute | solution.py:235
  79.1 17.1 %collective-permute-start.29 = (bf16[512,384]{1,0:T(8,128)(2,1)S(1)}, bf16[512,384]{1,0:T(8,128)(2,1)S(1)}, u32[]{:S(2)}, u32[]{:S(2)}) collective-permute-start(bf16[512,384]{1,0:T(8,128)(2,1)S(1)} %get-tuple-element.73), channel_id=1, source_target_pairs={{0,8},{8,0},{1,9},{9,1},{2,10},{10,2},{3,11},{11,3},{4,12},{12,4},... | collective-permute-start | bytes 1179656 | tf_op jit(solution)/shard_map/ppermute | solution.py:232
  82.6 9.0 %collective-permute-start.18 = (bf16[64,1536]{1,0:T(8,128)(2,1)S(1)}, bf16[64,1536]{1,0:T(8,128)(2,1)S(1)}, u32[]{:S(2)}, u32[]{:S(2)}) collective-permute-start(bf16[64,1536]{1,0:T(8,128)(2,1)S(1)} %collective-permute-done.16.refs_3_), channel_id=1, source_target_pairs={{0,16},{16,32},{32,48},{48,64},{64,80},{80,96},{96,112},{112,0},{8... | collective-permute-start | bytes 589832 | tf_op jit(solution)/shard_map/ppermute | solution.py:235
  86.8 9.0 %collective-permute-start.28 = (bf16[64,1536]{1,0:T(8,128)(2,1)S(1)}, bf16[64,1536]{1,0:T(8,128)(2,1)S(1)}, u32[]{:S(2)}, u32[]{:S(2)}) collective-permute-start(bf16[64,1536]{1,0:T(8,128)(2,1)S(1)} %collective-permute-done.26.refs_5_), channel_id=1, source_target_pairs={{0,16},{16,32},{32,48},{48,64},{64,80},{80,96},{96,112},{112,0},{8... | collective-permute-start | bytes 589832 | tf_op jit(solution)/shard_map/ppermute | solution.py:235
  97.4 9.0 %collective-permute-start.20 = (bf16[64,1536]{1,0:T(8,128)(2,1)S(1)}, bf16[64,1536]{1,0:T(8,128)(2,1)S(1)}, u32[]{:S(2)}, u32[]{:S(2)}) collective-permute-start(bf16[64,1536]{1,0:T(8,128)(2,1)S(1)} %collective-permute-done.18.refs_5_), channel_id=1, source_target_pairs={{0,16},{16,32},{32,48},{48,64},{64,80},{80,96},{96,112},{112,0},{8... | collective-permute-start | bytes 589832 | tf_op jit(solution)/shard_map/ppermute | solution.py:235
  101.8 17.2 %collective-permute-start.32 = (bf16[192,1536]{1,0:T(8,128)(2,1)}, bf16[192,1536]{1,0:T(8,128)(2,1)}, u32[]{:S(2)}, u32[]{:S(2)}) collective-permute-start(bf16[192,1536]{1,0:T(8,128)(2,1)} %get-tuple-element.74), channel_id=1, source_target_pairs={{0,128},{128,0},{1,129},{129,1},{2,130},{130,2},{3,131},{131,3},{4... | collective-permute-start | bytes 1769480 | tf_op jit(solution)/shard_map/ppermute | solution.py:325
  113.1 18.8 %collective-permute-start.31 = (bf16[384,1536]{1,0:T(8,128)(2,1)}, bf16[384,1536]{1,0:T(8,128)(2,1)S(1)}, u32[]{:S(2)}, u32[]{:S(2)}) collective-permute-start(bf16[384,1536]{1,0:T(8,128)(2,1)} %convolution_convert_fusion), channel_id=1, source_target_pairs={{0,8},{8,0},{1,9},{9,1},{2,10},{10,2},{3,11},{11,3},{4,12},{12,4},... | collective-permute-start | bytes 3538952 | tf_op jit(solution)/shard_map/ppermute | solution.py:232
  114.5 17.5 %collective-permute-start.33 = (bf16[192,1536]{1,0:T(8,128)(2,1)}, bf16[192,1536]{1,0:T(8,128)(2,1)}, u32[]{:S(2)}, u32[]{:S(2)}) collective-permute-start(bf16[192,1536]{1,0:T(8,128)(2,1)} %copy-done.2), channel_id=1, source_target_pairs={{0,128},{128,0},{1,129},{129,1},{2,130},{130,2},{3,131},{131,3},{4... | collective-permute-start | bytes 1769480 | tf_op jit(solution)/shard_map/ppermute | solution.py:325
  119.6 11.6 %collective-permute-start.35 = (bf16[2,128,384]{2,1,0:T(8,128)(2,1)S(1)}, bf16[2,128,384]{2,1,0:T(8,128)(2,1)S(1)}, u32[]{:S(2)}, u32[]{:S(2)}) collective-permute-start(bf16[2,128,384]{2,1,0:T(8,128)(2,1)S(1)} %get-tuple-element.95), channel_id=1, source_target_pairs={{0,1},{1,2},{2,3},{3,0},{4,5},{5,6},{6,7},{7,4},{8,9},{9,10},{10,1... | collective-permute-start | bytes 589832 | tf_op jit(solution)/shard_map/ppermute | solution.py:337
  120.6 10.7 %collective-permute-start.36 = (bf16[2,128,384]{2,1,0:T(8,128)(2,1)S(1)}, bf16[2,128,384]{2,1,0:T(8,128)(2,1)S(1)}, u32[]{:S(2)}, u32[]{:S(2)}) collective-permute-start(bf16[2,128,384]{2,1,0:T(8,128)(2,1)S(1)} %get-tuple-element.96), channel_id=1, source_target_pairs={{0,2},{1,3},{2,0},{3,1},{4,6},{5,7},{6,4},{7,5},{8,10},{9,11},{10,... | collective-permute-start | bytes 589832 | tf_op jit(solution)/shard_map/ppermute | solution.py:337
  122.7 9.2 %collective-permute-start.37 = (bf16[2,128,384]{2,1,0:T(8,128)(2,1)S(1)}, bf16[2,128,384]{2,1,0:T(8,128)(2,1)S(1)}, u32[]{:S(2)}, u32[]{:S(2)}) collective-permute-start(bf16[2,128,384]{2,1,0:T(8,128)(2,1)S(1)} %get-tuple-element.97), channel_id=1, source_target_pairs={{0,3},{1,0},{2,1},{3,2},{4,7},{5,4},{6,5},{7,6},{8,11},{9,8},{10,9... | collective-permute-start | bytes 589832 | tf_op jit(solution)/shard_map/ppermute | solution.py:337
  (27 other events, 154.7 us)
